TPU v7x, 256 devices: a whole 4x4x8 slice. The times are simulated.
256 devices in a mesh: tm: 16 (over z_lo, y, core), space: 16 (over z_hi, x).
Axes of the slice: x: 4, y: 4, z: 8 (z_hi: 4, z_lo: 2; z = z_hi * 2 + z_lo), core: 2. Of those that a mesh axis runs over, the one named last changes fastest.
Arguments:
- video: bfloat16 [64, 2048, 1152], P('tm', 'space'), may hold values from -4.9 to 4.9
- row_index: int32 [2048], P('space'), may hold values from 0 to 31, as said below
- col_index: int32 [2048], P('space'), may hold values from 0 to 63, as said below
- frame_index: int32 [64], P('tm'), may hold values from 0 to 95, as said below
- spatial_shift: float32 [1152], replicated, may hold values from -3 to 3
- spatial_scale: float32 [1152], replicated, may hold values from -0.5 to 0.5
- spatial_gate: float32 [1152], replicated, may hold values from 1 to 2
- spatial_qkv: bfloat16 [1152, 1728], replicated
- spatial_out: bfloat16 [576, 1152], replicated, may hold values from -0.25 to 0.25
- temporal_shift: float32 [1152], replicated, may hold values from -3 to 3
- temporal_scale: float32 [1152], replicated, may hold values from -0.5 to 0.5
- temporal_gate: float32 [1152], replicated, may hold values from 1 to 2
- temporal_qkv: bfloat16 [1152, 1728], replicated
- temporal_out: bfloat16 [576, 1152], replicated, may hold values from -0.25 to 0.25
Outputs:
- video_out: bfloat16 [64, 2048, 1152], P('tm', 'space')
Inputs may be any that keep to these rules, and one draw needn't show every extreme that they name: row_index * 64 + col_index takes every value of 0 to 2047 exactly once. `col_index`: see row_index. `frame_index`: starts at 0 and rises from each frame to the next by 1 or 2, by 2 in exactly 32 of the steps.
All inputs are finite; a program needn't handle non-finite values.
Results may differ from a plain program's by a relative error of at most 0.04.
Values may be sent and summed in bfloat16 or wider, within the bound.
A program may use at most 192 MiB of HBM per device.

v0:
```python
import math

import jax
import jax.numpy as jnp
from jax import lax
from jax.sharding import PartitionSpec as P

HEADS = 8
HD = 72


EPSILON = 1e-06


def normalize(stream):
    stream = stream.astype(jnp.float32)
    centre = stream - jnp.mean(stream, axis=-1, keepdims=True)
    spread = jnp.mean(centre * centre, axis=-1, keepdims=True)
    return centre * lax.rsqrt(spread + EPSILON)


def frequencies(pairs):
    return 10000.0 ** (-jnp.arange(pairs, dtype=jnp.float32) / pairs)


def rotate(vector, angles):
    half_size = vector.shape[-1] // 2
    leading = vector[..., :half_size]
    trailing = vector[..., half_size:]
    cosine = jnp.cos(angles)
    sines = jnp.sin(angles)
    return jnp.concatenate(
        [leading * cosine - trailing * sines, trailing * cosine + leading * sines], axis=-1
    )


def space_rotate(vector, row_angles, col_angles):
    half_size = vector.shape[-1] // 2
    return jnp.concatenate(
        [rotate(vector[..., :half_size], row_angles), rotate(vector[..., half_size:], col_angles)],
        axis=-1,
    )


def project(stream, shift, scale, weights):
    frames_here, patches_here, model_width = stream.shape
    modulated = (normalize(stream) * (1.0 + scale) + shift).astype(jnp.bfloat16)
    joined = jnp.dot(
        modulated.reshape(-1, model_width), weights, preferred_element_type=jnp.float32
    )
    return joined.reshape(frames_here, patches_here, 3, HEADS, HD)


def residual_add(stream, attended, gate, weights):
    frames_here, patches_here, model_width = stream.shape
    branch = jnp.dot(
        attended.reshape(frames_here * patches_here, -1),
        weights,
        preferred_element_type=jnp.float32,
    )
    return (stream.astype(jnp.float32) + gate * branch.reshape(stream.shape)).astype(jnp.bfloat16)


def body(
    video,
    row_index,
    col_index,
    frame_index,
    spatial_shift,
    spatial_scale,
    spatial_gate,
    spatial_qkv,
    spatial_out,
    temporal_shift,
    temporal_scale,
    temporal_gate,
    temporal_qkv,
    temporal_out,
):
    frames_here, patches_here, model_width = video.shape
    inv_root = 1.0 / math.sqrt(HD)
    row_angles = (row_index.astype(jnp.float32)[:, None] * frequencies(HD // 4))[None, :, None, :]
    col_angles = (col_index.astype(jnp.float32)[:, None] * frequencies(HD // 4))[None, :, None, :]
    time_angles = (frame_index.astype(jnp.float32)[:, None] * frequencies(HD // 2))[
        :, None, None, :
    ]
    joined = project(video, spatial_shift, spatial_scale, spatial_qkv)
    queries = space_rotate(joined[:, :, 0], row_angles, col_angles).astype(jnp.bfloat16)
    key_vectors = space_rotate(joined[:, :, 1], row_angles, col_angles).astype(jnp.bfloat16)
    value_vectors = joined[:, :, 2].astype(jnp.bfloat16)
    start_top = jnp.full((frames_here, HEADS, patches_here), -1e30, jnp.float32)
    run_top = start_top
    key_piece = lax.all_gather(key_vectors, "space", axis=1, tiled=True)
    value_piece = lax.all_gather(value_vectors, "space", axis=1, tiled=True)
    scores = (
        jnp.einsum("fphe,fkhe->fhpk", queries, key_piece, preferred_element_type=jnp.float32)
        * inv_root
    )
    new_top = jnp.maximum(run_top, jnp.max(scores, axis=-1))
    weights = jnp.exp(scores - new_top[..., None])
    run_sum = jnp.sum(weights, axis=-1)
    run_acc = jnp.einsum(
        "fhpk,fkhe->fhpe",
        weights.astype(jnp.bfloat16),
        value_piece,
        preferred_element_type=jnp.float32,
    )
    run_top, run_sum, run_acc = (new_top, run_sum, run_acc)
    attended = jnp.transpose(run_acc / run_sum[..., None], (0, 2, 1, 3)).astype(jnp.bfloat16)
    after = residual_add(video, attended, spatial_gate, spatial_out)
    joined = project(after, temporal_shift, temporal_scale, temporal_qkv)
    time_queries = rotate(joined[:, :, 0], time_angles).astype(jnp.bfloat16)
    time_keys = rotate(joined[:, :, 1], time_angles).astype(jnp.bfloat16)
    time_values = joined[:, :, 2].astype(jnp.bfloat16)
    frame_q = lax.all_to_all(time_queries, "tm", split_axis=1, concat_axis=0, tiled=True)
    frame_k = lax.all_to_all(time_keys, "tm", split_axis=1, concat_axis=0, tiled=True)
    frame_v = lax.all_to_all(time_values, "tm", split_axis=1, concat_axis=0, tiled=True)
    scores = (
        jnp.einsum("fphe,gphe->phfg", frame_q, frame_k, preferred_element_type=jnp.float32)
        * inv_root
    )
    row_top = jnp.max(scores, axis=-1, keepdims=True)
    weights = jnp.exp(scores - row_top)
    totals = jnp.sum(weights, axis=-1)
    mixed_out = jnp.einsum(
        "phfg,gphe->fphe", weights.astype(jnp.bfloat16), frame_v, preferred_element_type=jnp.float32
    )
    time_mixed = (mixed_out / jnp.transpose(totals, (2, 0, 1))[..., None]).astype(jnp.bfloat16)
    time_back = lax.all_to_all(time_mixed, "tm", split_axis=0, concat_axis=1, tiled=True)
    return residual_add(after, time_back, temporal_gate, temporal_out)


def solution(mesh):
    return jax.shard_map(
        body,
        mesh=mesh,
        in_specs=(
            P("tm", "space", None),
            P("space"),
            P("space"),
            P("tm"),
            P(),
            P(),
            P(),
            P(),
            P(),
            P(),
            P(),
            P(),
            P(),
            P(),
        ),
        out_specs=P("tm", "space", None),
        check_vma=False,
    )
```

profile of v0, /device:TPU:1, one launch (start us, length us, event | category | flops | bytes accessed | tf_op | source)
XLA Modules:
  0.0 417.6 jit_solution(7940040157760171951)
XLA Ops:
  6.5 0.0 copy-start
  6.5 0.0 all-gather.4.cloned.1.call-start
  6.6 1.6 convert_reduce_fusion.1
  8.3 1.7 fusion.17
  10.0 0.0 copy-done.9
  10.0 0.0 copy-done.1
  10.0 0.0 copy-done.12
  10.0 4.6 %fusion.42 = f32[4,128,3,8,72]{1,4,3,2,0:T(8,128)S(1)} fusion(bf16[3,8,72,1152,1]{3,2,1,0,4:T(8,128)(2,1)} %bitcast.100, bf16[4,128,1152]{2,1,0:T(8,128)(2,1)S(1)} %copy-done.1, f32[1152]{0:T(1024)S(1)} %copy-done.12, f32[1152]{0:T(1024)S(1)} %broadcast_add_fusion.1, f32[4,128]{1,0:T(4,128)S(1)} %add_rsqrt_fusion.1, f32[4,128]{1,0:T(4,128)S(1)} %broadcast_multiply_fusion.1), kind=kOutput, calls=%fused_computation.42 | convolution fusion | flops 2041970688 | bytes 8713216 | tf_op jit(solution)/shard_map/dot_general | solution.py:48
  14.6 0.0 copy-start.7
  14.7 0.0 copy-start.14
  14.7 0.0 copy-start.15
  14.7 1.3 slice_bitcast_fusion.3
  16.0 0.8 copy-done.7
  16.7 0.0 copy-done.14
  16.8 0.0 copy-done.15
  16.8 0.2 multiply_cosine_fusion.1
  16.9 0.3 subtract_convert_fusion.3
  17.2 0.0 copy-start.16
  17.2 0.0 copy-start.10
  17.3 1.1 pad_maximum_fusion
  18.3 0.0 all-gather.4.cloned.1.call-update
  18.3 0.2 all-gather.6.cloned.1.call-start
  18.6 2.2 slice.136
  20.8 0.0 all-gather.6.cloned.1.call-update
  20.8 0.1 multiply_cosine_fusion.2
  20.9 1.7 subtract_convert_fusion.5
  22.7 135.1 %all-gather.4.cloned.1.call-done = bf16[4,2048,8,72]{1,3,2,0:T(8,128)(2,1)} async-done(((bf16[4,128,8,72]{1,3,2,0:T(8,128)(2,1)}), bf16[4,2048,8,72]{1,3,2,0:T(8,128)(2,1)}) %all-gather.4.cloned.1.call-update) | async-done | bytes 9437200 | tf_op jit(solution)/shard_map/all_gather | solution.py:93
  157.8 16.0 %multiply_reduce_fusion = (f32[4,8,128]{2,1,0:T(8,128)S(1)}, f32[4,8,128,2048]{3,2,1,0:T(8,128)}) fusion(bf16[4,2048,8,72]{1,3,2,0:T(8,128)(2,1)} %all-gather.4.cloned.1.call-done, bf16[4,128,8,18]{1,3,2,0:T(8,128)(2,1)S(1)} %get-tuple-element.21, bf16[4,128,8,18]{1,3,2,0:T(8,128)(2,1)S(1)} %get-tuple-element.22, ...), kind=kOutput, calls=%fused_computation.1 | convolution fusion | flops 1227091968 | bytes 43597824 | tf_op jit(solution)/shard_map/fphe,fkhe->fhpk/dot_general | solution.py:96
  173.8 14.1 %fusion = f32[4,8,128]{2,1,0:T(8,128)S(1)} fusion(f32[4,8,128,2048]{3,2,1,0:T(8,128)} %get-tuple-element.36, f32[4,8,128]{2,1,0:T(8,128)S(1)} %broadcast_maximum_fusion), kind=kLoop, calls=%fused_computation.2 | loop fusion | flops 25161728 | bytes 33587200 | tf_op jit(solution)/shard_map/reduce_sum | solution.py:101
  187.9 106.8 %all-gather.6.cloned.1.call-done = bf16[4,2048,1,8,72]{1,4,3,2,0:T(8,128)(2,1)} async-done(((bf16[4,128,1,8,72]{1,4,3,2,0:T(8,128)(2,1)}), bf16[4,2048,1,8,72]{1,4,3,2,0:T(8,128)(2,1)}) %all-gather.6.cloned.1.call-update) | async-done | bytes 9437200 | tf_op jit(solution)/shard_map/all_gather | solution.py:94
  294.7 15.3 %fusion.36 = bf16[4,128,8,72]{1,3,2,0:T(8,128)(2,1)S(1)} fusion(bf16[4,2048,1,8,72]{1,4,3,2,0:T(8,128)(2,1)} %all-gather.6.cloned.1.call-done, f32[4,8,128,2048]{3,2,1,0:T(8,128)} %get-tuple-element.36, f32[4,8,128]{2,1,0:T(8,128)S(1)} %broadcast_maximum_fusion, f32[4,128,8]{1,2,0:T(8,128)S(1)} %bitcast.99), kind=kOutput, calls=%fused_computation.40 | convolution fusion | flops 1233715200 | bytes 43614208 | tf_op jit(solution)/shard_map/fhpk,fkhe->fhpe/dot_general | solution.py:102
  310.1 0.0 copy-start.11
  310.1 0.0 copy-start.13
  310.1 1.4 convert_reduce_fusion
  311.5 0.4 fusion.13
  312.0 0.2 copy-done.11
  312.2 2.8 fusion.45
  315.0 0.2 slice_bitcast_fusion
  315.1 1.6 copy-done.6
  316.7 1.3 subtract_convert_fusion
  318.0 0.1 pad_maximum_fusion.2
  318.1 1.7 copy.41
  319.8 4.7 %all-to-all-start.2 = ((bf16[4,128,8,72]{3,2,0,1:T(8,128)(2,1)}), bf16[4,128,8,72]{3,2,0,1:T(8,128)(2,1)S(1)}, u32[]{:S(2)}, u32[]{:S(2)}) async-start(bf16[4,128,8,72]{3,2,0,1:T(8,128)(2,1)} %copy.41), calls=%async_computation.2 | async-start | bytes 2097152 | tf_op jit(solution)/shard_map/all_to_all | solution.py:116
  324.5 1.1 pad_maximum_fusion.1
  325.6 1.7 copy.38
  327.3 13.0 %all-to-all-done.2 = bf16[4,128,8,72]{3,2,0,1:T(8,128)(2,1)S(1)} async-done(((bf16[4,128,8,72]{3,2,0,1:T(8,128)(2,1)}), bf16[4,128,8,72]{3,2,0,1:T(8,128)(2,1)S(1)}, u32[]{:S(2)}, u32[]{:S(2)}) %all-to-all-start.2) | async-done | bytes 589856 | tf_op jit(solution)/shard_map/all_to_all | solution.py:116
  340.3 4.3 %all-to-all-start.1 = ((bf16[4,128,8,72]{3,2,0,1:T(8,128)(2,1)}), bf16[4,128,8,72]{3,2,0,1:T(8,128)(2,1)S(1)}, u32[]{:S(2)}, u32[]{:S(2)}) async-start(bf16[4,128,8,72]{3,2,0,1:T(8,128)(2,1)} %copy.38), calls=%async_computation.1 | async-start | bytes 2097152 | tf_op jit(solution)/shard_map/all_to_all | solution.py:115
  344.7 2.2 fusion.58
  346.8 2.6 copy.34
  349.5 11.1 %all-to-all-done.1 = bf16[4,128,8,72]{3,2,0,1:T(8,128)(2,1)S(1)} async-done(((bf16[4,128,8,72]{3,2,0,1:T(8,128)(2,1)}), bf16[4,128,8,72]{3,2,0,1:T(8,128)(2,1)S(1)}, u32[]{:S(2)}, u32[]{:S(2)}) %all-to-all-start.1) | async-done | bytes 589856 | tf_op jit(solution)/shard_map/all_to_all | solution.py:115
  360.6 4.9 %all-to-all-start = ((bf16[4,128,8,72]{3,2,0,1:T(8,128)(2,1)}), bf16[4,128,8,72]{3,2,0,1:T(8,128)(2,1)}, u32[]{:S(2)}, u32[]{:S(2)}) async-start(bf16[4,128,8,72]{3,2,0,1:T(8,128)(2,1)} %copy.34), calls=%async_computation | async-start | bytes 2097152 | tf_op jit(solution)/shard_map/all_to_all | solution.py:117
  365.5 1.5 copy.43
  367.0 1.5 copy.40
  368.5 13.0 %all-to-all-done = bf16[4,128,8,72]{3,2,0,1:T(8,128)(2,1)} async-done(((bf16[4,128,8,72]{3,2,0,1:T(8,128)(2,1)}), bf16[4,128,8,72]{3,2,0,1:T(8,128)(2,1)}, u32[]{:S(2)}, u32[]{:S(2)}) %all-to-all-start) | async-done | bytes 589856 | tf_op jit(solution)/shard_map/all_to_all | solution.py:117
  381.5 1.8 copy.36
  383.3 0.7 multiply_reduce_fusion.1
  384.0 0.6 fusion.22
  384.6 1.2 fusion.21
  385.8 0.7 copy.45
  386.5 18.8 %all_to_all.69 = bf16[64,8,8,72]{3,2,1,0:T(8,128)(2,1)S(1)} all-to-all(bf16[64,8,8,72]{3,2,1,0:T(8,128)(2,1)S(1)} %copy.45), channel_id=1, replica_groups=mesh['tm'=16,'space'=16] {'tm'}, dimensions={0} | all-to-all | bytes 1179648 | tf_op jit(solution)/shard_map/all_to_all | solution.py:129
  405.3 0.1 copy.58
  405.4 1.7 dot_general.51
  407.1 0.0 copy-done.3
  407.1 3.7 fusion.8
  (29 shorter events, 0.1 us)
Async XLA Ops:
  6.5 303.5 %copy-start = (bf16[576,1152]{1,0:T(8,128)(2,1)S(1)}, bf16[576,1152]{1,0:T(8,128)(2,1)}, u32[]{:S(2)}) copy-start(bf16[576,1152]{1,0:T(8,128)(2,1)} %param.22) | copy-start | bytes 3981316
  6.5 3.5 copy-start.1
  6.5 3.4 copy-start.9
  6.5 3.5 copy-start.12
  6.5 151.2 %all-gather.4.cloned.1.call-start = ((), (), s32[]{:S(2)}) async-start(), calls=%async_computation.4 | async-start | bytes 10027008 | tf_op jit(solution)/shard_map/all_gather | solution.py:93
  14.6 2.1 copy-start.7
  14.7 2.1 copy-start.14
  14.7 2.1 copy-start.15
  17.2 3.5 copy-start.16
  17.2 3.7 copy-start.10
  18.3 276.4 %all-gather.6.cloned.1.call-start = ((), (), s32[]{:S(2)}) async-start(), calls=%async_computation.5 | async-start | bytes 10027008 | tf_op jit(solution)/shard_map/all_gather | solution.py:94
  294.7 15.3 %copy-start.8 = (f32[1152]{0:T(1024)S(1)}, f32[1152]{0:T(1024)}, u32[]{:S(2)}) copy-start(f32[1152]{0:T(1024)} %param.20) | copy-start | bytes 13828
  310.1 2.1 copy-start.11
  310.1 2.1 copy-start.13
  311.5 3.5 copy-start.2
  315.0 1.7 copy-start.6
  319.8 20.5 %all-to-all-start.2 = ((bf16[4,128,8,72]{3,2,0,1:T(8,128)(2,1)}), bf16[4,128,8,72]{3,2,0,1:T(8,128)(2,1)S(1)}, u32[]{:S(2)}, u32[]{:S(2)}) async-start(bf16[4,128,8,72]{3,2,0,1:T(8,128)(2,1)} %copy.41), calls=%async_computation.2 | async-start | bytes 2097152 | tf_op jit(solution)/shard_map/all_to_all | solution.py:116
  340.3 20.2 %all-to-all-start.1 = ((bf16[4,128,8,72]{3,2,0,1:T(8,128)(2,1)}), bf16[4,128,8,72]{3,2,0,1:T(8,128)(2,1)S(1)}, u32[]{:S(2)}, u32[]{:S(2)}) async-start(bf16[4,128,8,72]{3,2,0,1:T(8,128)(2,1)} %copy.38), calls=%async_computation.1 | async-start | bytes 2097152 | tf_op jit(solution)/shard_map/all_to_all | solution.py:115
  360.6 20.9 %all-to-all-start = ((bf16[4,128,8,72]{3,2,0,1:T(8,128)(2,1)}), bf16[4,128,8,72]{3,2,0,1:T(8,128)(2,1)}, u32[]{:S(2)}, u32[]{:S(2)}) async-start(bf16[4,128,8,72]{3,2,0,1:T(8,128)(2,1)} %copy.34), calls=%async_computation | async-start | bytes 2097152 | tf_op jit(solution)/shard_map/all_to_all | solution.py:117
  367.0 16.3 %copy-start.4 = (bf16[16,4,8,8,72]{4,1,0,3,2:T(4,128)(2,1)S(1)}, bf16[16,4,8,8,72]{4,1,0,3,2:T(4,128)(2,1)}, u32[]{:S(2)}) copy-start(bf16[16,4,8,8,72]{4,1,0,3,2:T(4,128)(2,1)} %copy.43) | copy-start | bytes 1769476
  368.5 14.8 %copy-start.5 = (bf16[16,4,8,8,72]{4,1,0,3,2:T(4,128)(2,1)S(1)}, bf16[16,4,8,8,72]{4,1,0,3,2:T(4,128)(2,1)}, u32[]{:S(2)}) copy-start(bf16[16,4,8,8,72]{4,1,0,3,2:T(4,128)(2,1)} %copy.40) | copy-start | bytes 1769476
  405.3 1.8 copy-start.3
Sparse Core Ops, SparseCore 0:
  18.5 139.2 all-gather.3
  160.2 134.5 all-gather.5
where the time goes:
time: 418 us
  waiting for transfers between devices  279 us (67%)
  matrix products  45.6 us (11%)
  other arithmetic  24.5 us (6%)
  local copies, waits for them, and re-layouts  21.8 us (5%)
  blocking collectives  18.8 us (4%)
  starting transfers between devices  14.2 us (3%)
  between operations  13.7 us (3%)
    all_gather x1, waiting for transfers between devices, body(): key_piece = lax.all_gather(key_vectors, 'space', axis=1, tiled=True)  135 us
    all_gather x1, waiting for transfers between devices, body(): value_piece = lax.all_gather(value_vectors, 'space', axis=1, tiled=True)  107 us
    all_to_all x1, blocking collectives, body(): lax.all_to_all(time_mixed, 'tm', split_axis=0, concat_axis=1, tiled=True)  18.8 us
    dot_general x1, matrix products, body(): jnp.einsum('fphe,fkhe->fhpk', queries, key_piece, preferred_element_type=...  16 us
    dot_general x1, matrix products, body(): jnp.einsum('fhpk,fkhe->fhpe', weights.astype(jnp.bfloat16), value_piece,...  15.3 us
    reduce_sum x1, other arithmetic, body(): run_sum = jnp.sum(weights, axis=-1)  14.1 us
    all_to_all x1, waiting for transfers between devices, body(): lax.all_to_all(time_keys, 'tm', split_axis=1, concat_axis=0, tiled=True)  13 us
    all_to_all x1, waiting for transfers between devices, body(): lax.all_to_all(time_values, 'tm', split_axis=1, concat_axis=0, tiled=True)  13 us
  transfers between devices with their start and end apart: 5, of which 5 were waited for; matrix products, arithmetic and copies ran while one was open for 11% of the time, Pallas kernels for 0%

commit v1 on v0

v1 whole, which is shorter than its diff:
```python
import functools
import math

import jax
import jax.numpy as jnp
import numpy as np
from jax import lax
from jax.experimental import pallas as pl
from jax.experimental.pallas import tpu as pltpu
from jax.sharding import PartitionSpec as P

HEADS = 8
HD = 72
D = 1152
INNER = HEADS * HD
FRAMES = 4
PATCHES = 128
SPACE = 16
PAIR = 2 * HD
EPSILON = 1e-06
MESH = pl.DeviceIdType.MESH
BF16 = jnp.bfloat16
F32 = jnp.float32


def normalize(stream):
    stream = stream.astype(jnp.float32)
    centre = stream - jnp.mean(stream, axis=-1, keepdims=True)
    spread = jnp.mean(centre * centre, axis=-1, keepdims=True)
    return centre * lax.rsqrt(spread + EPSILON)


def frequencies(pairs):
    return 10000.0 ** (-jnp.arange(pairs, dtype=jnp.float32) / pairs)


def rotate(vector, angles):
    half_size = vector.shape[-1] // 2
    leading = vector[..., :half_size]
    trailing = vector[..., half_size:]
    cosine = jnp.cos(angles)
    sines = jnp.sin(angles)
    return jnp.concatenate(
        [leading * cosine - trailing * sines, trailing * cosine + leading * sines], axis=-1
    )


def rotation_tables(angles, half):
    lane = lax.broadcasted_iota(jnp.int32, angles.shape, 1)
    leading = lax.rem(lane, 2 * half) < half
    cosine = jnp.cos(angles)
    sine = jnp.sin(angles)
    lead = jnp.where(leading, -sine, 0.0)
    trail = jnp.where(leading, 0.0, sine)
    return [jnp.concatenate([t] * (2 * HEADS), axis=1) for t in (cosine, lead, trail)]


def rotated(u, cosine, lead, trail, half):
    width = u.shape[1]
    ahead = pltpu.roll(u, width - half, 1)
    behind = pltpu.roll(u, half, 1)
    return u * cosine + ahead * lead + behind * trail


def space_kernel(
    video, pos, freq, shift, scale, w, out,
    send_kv, send_q, recv_kv, recv_q, send_o, key_a, key_b, value_t, tables,
    kv_ssem, kv_rsem, q_ssem, q_rsem, o_ssem, o_rsem, local_sem,
):
    me = lax.axis_index("space")
    zh = me // 4
    x = lax.rem(me, 4)

    barrier = pltpu.get_barrier_semaphore()
    for k in range(1, SPACE):
        other = lax.rem(me + k, SPACE)
        pl.semaphore_signal(barrier, 1, device_id={"space": other}, device_id_type=MESH)

    angles = pos[:, 0:1] * freq[0:1, :] + pos[:, 1:2] * freq[1:2, :]
    for i, t in enumerate(rotation_tables(angles, HD // 4)):
        tables[i] = t

    offsets = (2, 1, 3, 0)

    def project(i):
        f = lax.rem(zh + offsets[i], 4)
        y = jnp.dot(
            (normalize(video[f]) * (1.0 + scale[...]) + shift[...]).astype(BF16),
            w[...],
            preferred_element_type=F32,
        )
        turned = rotated(y[:, : 2 * INNER], tables[0], tables[1], tables[2], HD // 4)
        turned = jnp.transpose(turned).astype(BF16)
        values = jnp.transpose(y[:, 2 * INNER :]).astype(BF16)
        for c in range(4):
            r = slice(c * PAIR, (c + 1) * PAIR)
            send_q[i, c] = turned[r]
            send_kv[i, c, 0:PAIR] = turned[INNER + c * PAIR : INNER + (c + 1) * PAIR]
            send_kv[i, c, PAIR : 2 * PAIR] = values[r]

    def copy_to(i, k, src, dst, ssem, rsem):
        c = lax.rem(x + k, 4)
        f = lax.rem(zh + offsets[i], 4)
        return pltpu.make_async_remote_copy(
            src_ref=src.at[i, c],
            dst_ref=dst.at[me],
            send_sem=ssem.at[i, k],
            recv_sem=rsem.at[me],
            device_id={"space": f * 4 + c},
            device_id_type=MESH,
        )

    remote = [(i, k) for i in range(4) for k in (1, 3, 2, 0) if (i, k) != (3, 0)]
    project(0)
    pl.semaphore_wait(barrier, SPACE - 1)
    for i in range(4):
        if i:
            project(i)
        for k in (1, 3, 2, 0):
            if (i, k) in remote:
                copy_to(i, k, send_kv, recv_kv, kv_ssem, kv_rsem).start()
    for i, k in remote:
        copy_to(i, k, send_q, recv_q, q_ssem, q_rsem).start()

    lane = lax.broadcasted_iota(jnp.int32, (PATCHES, PAIR), 1)
    first = lane < HD
    value_t[PAIR:] = jnp.where(
        lax.broadcasted_iota(jnp.int32, (16, SPACE * PATCHES), 0) == 0, 1.0, 0.0
    ).astype(BF16)

    def place(kv, j):
        rows = pl.ds(pl.multiple_of(j * PATCHES, PATCHES), PATCHES)
        keys = jnp.transpose(kv[0:PAIR].astype(F32))
        key_a[rows] = jnp.where(first, keys, 0.0).astype(BF16)
        key_b[rows] = jnp.where(first, 0.0, keys).astype(BF16)
        value_t[0:PAIR, rows] = kv[PAIR : 2 * PAIR]

    place(send_kv[3, x], me)
    recv_q[me] = send_q[3, x]

    def source(n):
        i = n // 4
        off = jnp.where(i == 0, 2, jnp.where(i == 1, 3, jnp.where(i == 2, 1, 0)))
        return lax.rem(zh + off, 4) * 4 + lax.rem(x + 1 + lax.rem(n, 4), 4)

    def arrive(n, carry):
        j = source(n)
        pltpu.make_async_remote_copy(
            src_ref=send_kv.at[0, 0], dst_ref=recv_kv.at[j], send_sem=kv_ssem.at[0, 0],
            recv_sem=kv_rsem.at[j], device_id={"space": j}, device_id_type=MESH,
        ).wait_recv()
        place(recv_kv[j], j)
        return carry

    lax.fori_loop(0, SPACE - 1, arrive, 0)

    def wait_q(n, carry):
        j = source(n)
        pltpu.make_async_remote_copy(
            src_ref=send_q.at[0, 0], dst_ref=recv_q.at[j], send_sem=q_ssem.at[0, 0],
            recv_sem=q_rsem.at[j], device_id={"space": j}, device_id_type=MESH,
        ).wait_recv()
        return carry

    lax.fori_loop(0, SPACE - 1, wait_q, 0)

    factor = math.log2(math.e) / math.sqrt(HD)
    row = lax.broadcasted_iota(jnp.int32, (PAIR, 2 * PATCHES), 0)

    def o_copy(j):
        return pltpu.make_async_remote_copy(
            src_ref=send_o.at[j],
            dst_ref=out.at[me],
            send_sem=o_ssem.at[j],
            recv_sem=o_rsem.at[me],
            device_id={"space": j},
            device_id_type=MESH,
        )

    def attend(n, carry):
        b = lax.rem(me // 2 + 1 + n, SPACE // 2)
        queries = jnp.concatenate([recv_q[2 * b], recv_q[2 * b + 1]], axis=1)
        mixed = []
        for keys in (key_a, key_b):
            scores = jnp.dot(keys[...], queries, preferred_element_type=F32)
            top = jnp.max(scores, axis=0, keepdims=True)
            weights = jnp.exp2((scores - top) * factor).astype(BF16)
            both = jnp.dot(value_t[...], weights, preferred_element_type=F32)
            mixed.append(both[0:PAIR] / both[PAIR : PAIR + 1])
        result = jnp.where(row < HD, mixed[0], mixed[1]).astype(BF16)
        for e in range(2):
            j = 2 * b + e
            send_o[j] = result[:, e * PATCHES : (e + 1) * PATCHES]

            @pl.when(j != me)
            def _():
                o_copy(j).start()

        return carry

    lax.fori_loop(0, SPACE // 2, attend, 0)
    own = pltpu.make_async_copy(send_o.at[me], out.at[me], local_sem)
    own.start()
    own.wait()

    for i, k in remote:
        copy_to(i, k, send_kv, recv_kv, kv_ssem, kv_rsem).wait_send()
        copy_to(i, k, send_q, recv_q, q_ssem, q_rsem).wait_send()

    def finish(n, carry):
        j = lax.rem(me + 1 + n, SPACE)
        o_copy(j).wait_send()
        pltpu.make_async_remote_copy(
            src_ref=send_o.at[j], dst_ref=out.at[j], send_sem=o_ssem.at[j],
            recv_sem=o_rsem.at[j], device_id={"space": j}, device_id_type=MESH,
        ).wait_recv()
        return carry

    lax.fori_loop(0, SPACE - 1, finish, 0)


def space_attention(video, pos, freq, shift, scale, w):
    vmem = pl.BlockSpec(memory_space=pltpu.VMEM)
    dma = pltpu.SemaphoreType.DMA
    tokens = SPACE * PATCHES
    return pl.pallas_call(
        space_kernel,
        out_shape=jax.ShapeDtypeStruct((SPACE, PAIR, PATCHES), BF16),
        in_specs=[vmem] * 6,
        out_specs=vmem,
        scratch_shapes=[
            pltpu.VMEM((4, 4, 2 * PAIR, PATCHES), BF16),
            pltpu.VMEM((4, 4, PAIR, PATCHES), BF16),
            pltpu.VMEM((SPACE, 2 * PAIR, PATCHES), BF16),
            pltpu.VMEM((SPACE, PAIR, PATCHES), BF16),
            pltpu.VMEM((SPACE, PAIR, PATCHES), BF16),
            pltpu.VMEM((tokens, PAIR), BF16),
            pltpu.VMEM((tokens, PAIR), BF16),
            pltpu.VMEM((PAIR + 16, tokens), BF16),
            pltpu.VMEM((3, PATCHES, 2 * INNER), F32),
            dma((4, 4)), dma((SPACE,)), dma((4, 4)), dma((SPACE,)), dma((SPACE,)), dma((SPACE,)), dma,
        ],
        compiler_params=pltpu.CompilerParams(
            collective_id=1, has_side_effects=True, vmem_limit_bytes=52 * 2**20
        ),
        name="space_attention",
    )(video, pos, freq, shift, scale, w)


def project(stream, shift, scale, weights):
    frames_here, patches_here, model_width = stream.shape
    modulated = (normalize(stream) * (1.0 + scale) + shift).astype(jnp.bfloat16)
    joined = jnp.dot(
        modulated.reshape(-1, model_width), weights, preferred_element_type=jnp.float32
    )
    return joined.reshape(frames_here, patches_here, 3, HEADS, HD)


def residual_add(stream, attended, gate, weights):
    frames_here, patches_here, model_width = stream.shape
    branch = jnp.dot(
        attended.reshape(frames_here * patches_here, -1),
        weights,
        preferred_element_type=jnp.float32,
    )
    return (stream.astype(jnp.float32) + gate * branch.reshape(stream.shape)).astype(jnp.bfloat16)


def space_frequencies():
    f = 10000.0 ** (-np.arange(HD // 4, dtype=np.float32) / (HD // 4))
    zero = np.zeros_like(f)
    table = np.zeros((8, HD), np.float32)
    table[0] = np.concatenate([f, f, zero, zero])
    table[1] = np.concatenate([zero, zero, f, f])
    return jnp.asarray(table)


def body(
    video,
    row_index,
    col_index,
    frame_index,
    spatial_shift,
    spatial_scale,
    spatial_gate,
    spatial_qkv,
    spatial_out,
    temporal_shift,
    temporal_scale,
    temporal_gate,
    temporal_qkv,
    temporal_out,
):
    inv_root = 1.0 / math.sqrt(HD)
    pos = jnp.stack([row_index, col_index], axis=1).astype(F32)
    attended = space_attention(
        video, pos, space_frequencies(), spatial_shift[None], spatial_scale[None], spatial_qkv
    )
    attended = jnp.transpose(attended.reshape(FRAMES, INNER, PATCHES), (0, 2, 1))
    after = residual_add(video, attended, spatial_gate, spatial_out)
    time_angles = (frame_index.astype(jnp.float32)[:, None] * frequencies(HD // 2))[
        :, None, None, :
    ]
    joined = project(after, temporal_shift, temporal_scale, temporal_qkv)
    time_queries = rotate(joined[:, :, 0], time_angles).astype(jnp.bfloat16)
    time_keys = rotate(joined[:, :, 1], time_angles).astype(jnp.bfloat16)
    time_values = joined[:, :, 2].astype(jnp.bfloat16)
    frame_q = lax.all_to_all(time_queries, "tm", split_axis=1, concat_axis=0, tiled=True)
    frame_k = lax.all_to_all(time_keys, "tm", split_axis=1, concat_axis=0, tiled=True)
    frame_v = lax.all_to_all(time_values, "tm", split_axis=1, concat_axis=0, tiled=True)
    scores = (
        jnp.einsum("fphe,gphe->phfg", frame_q, frame_k, preferred_element_type=jnp.float32)
        * inv_root
    )
    row_top = jnp.max(scores, axis=-1, keepdims=True)
    weights = jnp.exp(scores - row_top)
    totals = jnp.sum(weights, axis=-1)
    mixed_out = jnp.einsum(
        "phfg,gphe->fphe", weights.astype(jnp.bfloat16), frame_v, preferred_element_type=jnp.float32
    )
    time_mixed = (mixed_out / jnp.transpose(totals, (2, 0, 1))[..., None]).astype(jnp.bfloat16)
    time_back = lax.all_to_all(time_mixed, "tm", split_axis=0, concat_axis=1, tiled=True)
    return residual_add(after, time_back, temporal_gate, temporal_out)


def solution(mesh):
    return jax.shard_map(
        body,
        mesh=mesh,
        in_specs=(P("tm", "space", None), P("space"), P("space"), P("tm")) + (P(),) * 10,
        out_specs=P("tm", "space", None),
        check_vma=False,
    )
```

time: 418 us -> 195 us (0.47)
  waiting for transfers between devices: 279 us -> 37 us
  Pallas kernels: 0 us -> 78.8 us
  matrix products: 45.6 us -> 9.68 us
  other arithmetic: 24.5 us -> 6.81 us
  between operations: 13.7 us -> 0.18 us
    all_gather x2 -> x0, waiting for transfers between devices: 242 us -> none  [the longest x1 135 us: body(): key_piece = lax.all_gather(key_vectors, 'space', axis=1, tiled=True)]
    pallas_call x0 -> x1, Pallas kernels: none -> 78.8 us  [space_attention(): pl.pallas_call(space_kernel, out_shape=jax.ShapeDtypeStruct((SPACE, PAIR,...]
    dot_general x2 -> x0, matrix products: 31.3 us -> none  [the longest x1 16 us: body(): jnp.einsum('fphe,fkhe->fhpk', queries, key_piece, preferred_element_type=...]
    reduce_sum x2 -> x0, other arithmetic: 15.8 us -> none  [the longest x1 14.1 us: body(): run_sum = jnp.sum(weights, axis=-1)]
    unnamed x34 -> x23, local copies, waits for them, and re-layouts: 2.67 us -> 9.05 us
    dot_general x2 -> x1, matrix products: 7.38 us -> 2.77 us  [project(): jnp.dot(modulated.reshape(-1, model_width), weights, preferred_element_ty...]
  transfers between devices with their start and end apart: 5 -> 3, of which waited for: 5 -> 3; matrix products, arithmetic and copies ran while one was open for 11% -> 6% of each run, Pallas kernels for 0% -> 0%
where the time goes in v1:
time: 195 us; the launch traced here: 191 us
  Pallas kernels  78.8 us (40%)
  waiting for transfers between devices  37 us (19%)
  local copies, waits for them, and re-layouts  25.4 us (13%)
  blocking collectives  18.8 us (10%)
  starting transfers between devices  14.8 us (8%)
  matrix products  9.68 us (5%)
  other arithmetic  6.81 us (3%)
    pallas_call x1, Pallas kernels, space_attention(): pl.pallas_call(space_kernel, out_shape=jax.ShapeDtypeStruct((SPACE, PAIR,...  78.8 us
    all_to_all x1, blocking collectives, body(): lax.all_to_all(time_mixed, 'tm', split_axis=0, concat_axis=1, tiled=True)  18.8 us
    all_to_all x1, waiting for transfers between devices, body(): lax.all_to_all(time_queries, 'tm', split_axis=1, concat_axis=0, tiled=True)  12.9 us
    all_to_all x1, waiting for transfers between devices, body(): lax.all_to_all(time_keys, 'tm', split_axis=1, concat_axis=0, tiled=True)  12.8 us
    all_to_all x1, waiting for transfers between devices, body(): lax.all_to_all(time_values, 'tm', split_axis=1, concat_axis=0, tiled=True)  11.3 us
    unnamed x23, local copies, waits for them, and re-layouts  9.05 us
    all_to_all x1, starting transfers between devices, body(): lax.all_to_all(time_keys, 'tm', split_axis=1, concat_axis=0, tiled=True)  5.52 us
    dot_general x2, matrix products, residual_add(): jnp.dot(attended.reshape(frames_here * patches_here, -1), weights, prefer...  5.04 us
  transfers between devices with their start and end apart: 3, of which 3 were waited for; matrix products, arithmetic and copies ran while one was open for 6% of the time, Pallas kernels for 0%

profile of v1, /device:TPU:1, one launch (start us, length us, event | category | flops | bytes accessed | tf_op | source)
XLA Modules:
  0.0 191.5 jit_solution(11975035905365037062)
XLA Ops:
  0.0 0.0 copy-start
  0.0 0.8 convert_element_type.40
  0.8 0.7 broadcast_in_dim.4.shift
  1.5 0.7 broadcast_in_dim.5.scale
  2.2 0.7 broadcast_add_fusion
  2.9 0.7 add_convert_fusion.2
  3.6 0.1 copy.54.pos
  3.7 0.0 copy-start.1
  3.7 0.0 copy-start.2
  3.7 6.6 %copy.55.w = bf16[1152,1728]{1,0:T(8,128)(2,1)} copy(bf16[1152,1728]{0,1:T(8,128)(2,1)} %param.22) | data formatting | bytes 7962624 | tf_op args[7]
  10.2 0.0 copy-done.1
  10.2 0.0 copy-done.2
  10.3 0.0 copy-start.8
  10.3 78.8 %space_attention.1 = bf16[16,144,128]{2,1,0:T(8,128)(2,1)S(1)} custom-call(bf16[4,128,1152]{2,1,0:T(8,128)(2,1)S(1)} %copy-done.1, f32[128,2]{1,0:T(8,128)S(1)} %copy.54.pos, f32[8,72]{1,0:T(8,128)S(1)} %copy-done.2, f32[1,1152]{1,0:T(1,128)S(1)} %broadcast_in_dim.4.shift, f32[1,1152]{1,0:T(1,128)S(1)} %broadcast_in_dim.5.scale, bf16[1152,1728]{1,0:T(8,128)(2,1)} %copy.55.w), custom_call_target="tpu_custom_call" | custom-call | tf_op jit(solution)/shard_map/space_attention/pallas_call | solution.py:226
  89.1 0.0 copy-done
  89.1 0.0 copy-done.8
  89.1 0.0 copy-start.9
  89.1 0.0 copy-start.10
  89.1 1.4 convert_reduce_fusion
  90.5 0.0 copy-start.3
  90.5 0.4 fusion.5
  91.0 0.2 copy-done.9
  91.2 0.0 copy-done.10
  91.2 2.8 %fusion.15 = f32[4,128,3,8,72]{1,4,3,2,0:T(8,128)S(1)} fusion(bf16[3,8,72,1152,1]{3,2,1,0,4:T(8,128)(2,1)S(1)} %bitcast.71, bf16[4,128,1152]{2,1,0:T(8,128)(2,1)S(1)} %get-tuple-element.16, f32[1152]{0:T(1024)S(1)} %copy-done.10, f32[1152]{0:T(1024)S(1)} %broadcast_add_fusion, f32[4,128]{1,0:T(4,128)S(1)} %add_rsqrt_fusion, ...), kind=kOutput, calls=%fused_computation.23 | convolution fusion | flops 2041970688 | bytes 8713216 | tf_op jit(solution)/shard_map/dot_general | solution.py:253
  94.0 0.0 copy-done.3
  94.0 0.0 copy-start.6
  94.0 0.2 slice_bitcast_fusion
  94.2 1.6 copy-done.6
  95.8 0.1 multiply_cosine_fusion
  95.9 1.4 subtract_convert_fusion
  97.2 0.1 pad_maximum_fusion.1
  97.4 1.7 copy.63
  99.1 5.5 %all-to-all-start.2 = ((bf16[4,128,8,72]{3,2,0,1:T(8,128)(2,1)}), bf16[4,128,8,72]{3,2,0,1:T(8,128)(2,1)S(1)}, u32[]{:S(2)}, u32[]{:S(2)}) async-start(bf16[4,128,8,72]{3,2,0,1:T(8,128)(2,1)} %copy.63), calls=%async_computation.2 | async-start | bytes 2097152 | tf_op jit(solution)/shard_map/all_to_all | solution.py:309
  104.6 1.3 fusion.24
  105.9 1.7 copy.56
  107.6 12.8 %all-to-all-done.2 = bf16[4,128,8,72]{3,2,0,1:T(8,128)(2,1)S(1)} async-done(((bf16[4,128,8,72]{3,2,0,1:T(8,128)(2,1)}), bf16[4,128,8,72]{3,2,0,1:T(8,128)(2,1)S(1)}, u32[]{:S(2)}, u32[]{:S(2)}) %all-to-all-start.2) | async-done | bytes 589856 | tf_op jit(solution)/shard_map/all_to_all | solution.py:309
  120.4 4.3 %all-to-all-start = ((bf16[4,128,8,72]{3,2,0,1:T(8,128)(2,1)}), bf16[4,128,8,72]{3,2,0,1:T(8,128)(2,1)S(1)}, u32[]{:S(2)}, u32[]{:S(2)}) async-start(bf16[4,128,8,72]{3,2,0,1:T(8,128)(2,1)} %copy.56), calls=%async_computation | async-start | bytes 2097152 | tf_op jit(solution)/shard_map/all_to_all | solution.py:310
  124.7 2.0 %pad_maximum_fusion = bf16[4,128,8,72]{1,3,2,0:T(8,128)(2,1)} fusion(bf16[4,128,8,36]{1,3,2,0:T(8,128)(2,1)} %get-tuple-element.11, bf16[4,128,8,36]{1,3,2,0:T(8,128)(2,1)} %get-tuple-element.12), kind=kLoop, calls=%fused_computation.39 | loop fusion | flops 1179648 | bytes 1179648 | tf_op jit(solution)/shard_map/concatenate | solution.py:43
  126.8 2.6 %copy.60 = bf16[4,128,8,72]{3,2,0,1:T(8,128)(2,1)} copy(bf16[4,128,8,72]{1,3,2,0:T(8,128)(2,1)} %pad_maximum_fusion) | data formatting | bytes 1179648 | tf_op jit(solution)/shard_map/concatenate | solution.py:43
  129.4 11.3 %all-to-all-done = bf16[4,128,8,72]{3,2,0,1:T(8,128)(2,1)S(1)} async-done(((bf16[4,128,8,72]{3,2,0,1:T(8,128)(2,1)}), bf16[4,128,8,72]{3,2,0,1:T(8,128)(2,1)S(1)}, u32[]{:S(2)}, u32[]{:S(2)}) %all-to-all-start) | async-done | bytes 589856 | tf_op jit(solution)/shard_map/all_to_all | solution.py:310
  140.6 4.9 %all-to-all-start.1 = ((bf16[4,128,8,72]{3,2,0,1:T(8,128)(2,1)}), bf16[4,128,8,72]{3,2,0,1:T(8,128)(2,1)}, u32[]{:S(2)}, u32[]{:S(2)}) async-start(bf16[4,128,8,72]{3,2,0,1:T(8,128)(2,1)} %copy.60), calls=%async_computation.1 | async-start | bytes 2097152 | tf_op jit(solution)/shard_map/all_to_all | solution.py:308
  145.6 1.5 copy.65
  147.1 0.0 copy-start.5
  147.1 1.5 copy.58
  148.7 12.9 %all-to-all-done.1 = bf16[4,128,8,72]{3,2,0,1:T(8,128)(2,1)} async-done(((bf16[4,128,8,72]{3,2,0,1:T(8,128)(2,1)}), bf16[4,128,8,72]{3,2,0,1:T(8,128)(2,1)}, u32[]{:S(2)}, u32[]{:S(2)}) %all-to-all-start.1) | async-done | bytes 589856 | tf_op jit(solution)/shard_map/all_to_all | solution.py:308
  161.6 1.8 copy.62
  163.4 0.0 copy-done.5
  163.4 0.7 multiply_reduce_fusion
  164.1 0.0 copy-start.7
  164.1 0.6 fusion.10
  164.7 0.6 copy-done.7
  165.4 1.2 fusion.9
  166.5 0.7 copy.67
  167.2 18.8 %all_to_all.69 = bf16[64,8,8,72]{3,2,1,0:T(8,128)(2,1)S(1)} all-to-all(bf16[64,8,8,72]{3,2,1,0:T(8,128)(2,1)S(1)} %copy.67), channel_id=1, replica_groups=mesh['tm'=16,'space'=16] {'tm'}, dimensions={0} | all-to-all | bytes 1179648 | tf_op jit(solution)/shard_map/all_to_all | solution.py:322
  186.0 0.0 copy-start.4
  186.0 0.1 copy.78
  186.1 1.7 dot_general.27
  187.8 0.0 copy-done.4
  187.8 3.7 %fusion.2 = bf16[4,128,1152]{2,1,0:T(8,128)(2,1)} fusion(bf16[4,128,576]{2,1,0:T(8,128)(2,1)} %dot_general.27, bf16[4,128,1152]{2,1,0:T(8,128)(2,1)S(1)} %copy-done.4, bf16[576,1152]{1,0:T(8,128)(2,1)} %param.28, f32[1152]{0:T(1024)} %param.26), kind=kOutput, calls=%fused_computation.7 | convolution fusion | flops 681836544 | bytes 4280832 | tf_op jit(solution)/shard_map/dot_general | solution.py:261
  (3 shorter events, 0.0 us)
Async XLA Ops:
  0.0 89.1 %copy-start = (bf16[576,1152]{1,0:T(8,128)(2,1)S(1)}, bf16[576,1152]{1,0:T(8,128)(2,1)}, u32[]{:S(2)}) copy-start(bf16[576,1152]{1,0:T(8,128)(2,1)} %param.23) | copy-start | bytes 3981316
  3.7 6.6 %copy-start.1 = (bf16[4,128,1152]{2,1,0:T(8,128)(2,1)S(1)}, bf16[4,128,1152]{2,1,0:T(8,128)(2,1)}, u32[]{:S(2)}) copy-start(bf16[4,128,1152]{2,1,0:T(8,128)(2,1)} %video.1) | copy-start | bytes 3538948
  3.7 6.6 %copy-start.2 = (f32[8,72]{1,0:T(8,128)S(1)}, f32[8,72]{1,0:T(8,128)}, u32[]{:S(2)}) copy-start(f32[8,72]{1,0:T(8,128)} %constant.21.clone.freq) | copy-start | bytes 6916
  10.3 78.8 %copy-start.8 = (f32[1152]{0:T(1024)S(1)}, f32[1152]{0:T(1024)}, u32[]{:S(2)}) copy-start(f32[1152]{0:T(1024)} %param.21) | copy-start | bytes 13828
  89.1 2.1 %copy-start.9 = (bf16[1152,1728]{0,1:T(8,128)(2,1)S(1)}, bf16[1152,1728]{0,1:T(8,128)(2,1)}, u32[]{:S(2)}) copy-start(bf16[1152,1728]{0,1:T(8,128)(2,1)} %param.27) | copy-start | bytes 11943940
  89.1 2.1 %copy-start.10 = (f32[1152]{0:T(1024)S(1)}, f32[1152]{0:T(1024)}, u32[]{:S(2)}) copy-start(f32[1152]{0:T(1024)} %param.24) | copy-start | bytes 13828
  90.5 3.5 %copy-start.3 = (bf16[4,128,1152]{2,1,0:T(8,128)(2,1)}, bf16[4,128,1152]{2,1,0:T(8,128)(2,1)S(1)}, u32[]{:S(2)}) copy-start(bf16[4,128,1152]{2,1,0:T(8,128)(2,1)S(1)} %get-tuple-element.16) | copy-start | bytes 3538948
  94.0 1.8 copy-start.6
  99.1 21.3 %all-to-all-start.2 = ((bf16[4,128,8,72]{3,2,0,1:T(8,128)(2,1)}), bf16[4,128,8,72]{3,2,0,1:T(8,128)(2,1)S(1)}, u32[]{:S(2)}, u32[]{:S(2)}) async-start(bf16[4,128,8,72]{3,2,0,1:T(8,128)(2,1)} %copy.63), calls=%async_computation.2 | async-start | bytes 2097152 | tf_op jit(solution)/shard_map/all_to_all | solution.py:309
  120.4 20.2 %all-to-all-start = ((bf16[4,128,8,72]{3,2,0,1:T(8,128)(2,1)}), bf16[4,128,8,72]{3,2,0,1:T(8,128)(2,1)S(1)}, u32[]{:S(2)}, u32[]{:S(2)}) async-start(bf16[4,128,8,72]{3,2,0,1:T(8,128)(2,1)} %copy.56), calls=%async_computation | async-start | bytes 2097152 | tf_op jit(solution)/shard_map/all_to_all | solution.py:310
  140.6 21.0 %all-to-all-start.1 = ((bf16[4,128,8,72]{3,2,0,1:T(8,128)(2,1)}), bf16[4,128,8,72]{3,2,0,1:T(8,128)(2,1)}, u32[]{:S(2)}, u32[]{:S(2)}) async-start(bf16[4,128,8,72]{3,2,0,1:T(8,128)(2,1)} %copy.60), calls=%async_computation.1 | async-start | bytes 2097152 | tf_op jit(solution)/shard_map/all_to_all | solution.py:308
  147.1 16.3 %copy-start.5 = (bf16[16,4,8,8,72]{4,1,0,3,2:T(4,128)(2,1)S(1)}, bf16[16,4,8,8,72]{4,1,0,3,2:T(4,128)(2,1)}, u32[]{:S(2)}) copy-start(bf16[16,4,8,8,72]{4,1,0,3,2:T(4,128)(2,1)} %copy.65) | copy-start | bytes 1769476
  164.1 1.2 copy-start.7
  186.0 1.8 copy-start.4

commit v2 on v1

v2 whole, which is shorter than its diff:
```python
import math

import jax
import jax.numpy as jnp
import numpy as np
from jax import lax
from jax.experimental import pallas as pl
from jax.experimental.pallas import tpu as pltpu
from jax.sharding import PartitionSpec as P

HEADS = 8
HD = 72
D = 1152
INNER = HEADS * HD
FRAMES = 4
PATCHES = 128
SPACE = 16
PAIR = 2 * HD
TM = 16
HALF = INNER % 128
WIDE = INNER + HALF
LANES = 3 * INNER + HALF
EPSILON = 1e-06
MESH = pl.DeviceIdType.MESH
BF16 = jnp.bfloat16
F32 = jnp.float32


def normalize(stream):
    stream = stream.astype(jnp.float32)
    centre = stream - jnp.mean(stream, axis=-1, keepdims=True)
    spread = jnp.mean(centre * centre, axis=-1, keepdims=True)
    return centre * lax.rsqrt(spread + EPSILON)


def rotated(u, cosine, lead, trail, half, axis):
    ahead = pltpu.roll(u, u.shape[axis] - half, axis)
    behind = pltpu.roll(u, half, axis)
    return u * cosine + ahead * lead + behind * trail


def space_kernel(
    video, pos, table, shift, scale, w, out,
    send_kv, send_q, recv_kv, recv_q, send_o, key_a, key_b, value_t, w_held,
    kv_ssem, kv_rsem, q_ssem, q_rsem, o_ssem, o_rsem, local_sem, w_sem,
):
    me = lax.axis_index("space")
    zh = me // 4
    x = lax.rem(me, 4)

    barrier = pltpu.get_barrier_semaphore()
    for k in range(1, SPACE):
        other = lax.rem(me + k, SPACE)
        pl.semaphore_signal(barrier, 1, device_id={"space": other}, device_id_type=MESH)

    loads = []
    for n in range(3):
        part = pl.ds(n * INNER, INNER)
        loads.append(pltpu.make_async_copy(w.at[part], w_held.at[part], w_sem.at[n]))
        loads[-1].start()

    angles = table[:, 0:1] * pos[0:1, :] + table[:, 1:2] * pos[1:2, :]
    cosine = jnp.cos(angles)
    sine = jnp.sin(angles)
    lead = sine * table[:, 2:3]
    trail = sine * table[:, 3:4]

    offsets = (2, 1, 3, 0)

    def project(i):
        frames = [lax.rem(zh + offsets[i + e], 4) for e in range(2)]
        mixed = [
            (normalize(video[f]) * (1.0 + scale[...]) + shift[...]).astype(BF16) for f in frames
        ]
        mixed = jnp.concatenate(mixed, axis=0)
        if i == 0:
            for load in loads:
                load.wait()
        y = lax.dot_general(
            w_held[...], mixed, (((1,), (1,)), ((), ())), preferred_element_type=F32
        )

        def turned(n, e):
            u = y[n * HD : (n + 1) * HD, e * PATCHES : (e + 1) * PATCHES]
            return rotated(u, cosine, lead, trail, HD // 4, 0)

        for e in range(2):
            for c in range(4):
                first = 2 * c
                send_q[i + e, c] = jnp.concatenate(
                    [turned(first, e), turned(first + 1, e)], axis=0
                ).astype(BF16)
                send_kv[i + e, c, 0:PAIR] = jnp.concatenate(
                    [turned(HEADS + first, e), turned(HEADS + first + 1, e)], axis=0
                ).astype(BF16)
                rows = slice(2 * INNER + c * PAIR, 2 * INNER + (c + 1) * PAIR)
                send_kv[i + e, c, PAIR : 2 * PAIR] = y[
                    rows, e * PATCHES : (e + 1) * PATCHES
                ].astype(BF16)

    def copy_to(i, k, src, dst, ssem, rsem):
        c = lax.rem(x + k, 4)
        f = lax.rem(zh + offsets[i], 4)
        return pltpu.make_async_remote_copy(
            src_ref=src.at[i, c],
            dst_ref=dst.at[me],
            send_sem=ssem.at[i, k],
            recv_sem=rsem.at[me],
            device_id={"space": f * 4 + c},
            device_id_type=MESH,
        )

    remote = [(i, k) for i in range(4) for k in (1, 3, 2, 0) if (i, k) != (3, 0)]
    project(0)
    pl.semaphore_wait(barrier, SPACE - 1)
    for i in range(4):
        if i == 2:
            project(i)
        for k in (1, 3, 2, 0):
            if (i, k) in remote:
                copy_to(i, k, send_kv, recv_kv, kv_ssem, kv_rsem).start()
    for i, k in remote:
        copy_to(i, k, send_q, recv_q, q_ssem, q_rsem).start()

    lane = lax.broadcasted_iota(jnp.int32, (PATCHES, PAIR), 1)
    first = lane < HD
    value_t[PAIR:] = jnp.where(
        lax.broadcasted_iota(jnp.int32, (16, SPACE * PATCHES), 0) == 0, 1.0, 0.0
    ).astype(BF16)

    def place(kv, j):
        rows = pl.ds(pl.multiple_of(j * PATCHES, PATCHES), PATCHES)
        keys = jnp.transpose(kv[0:PAIR].astype(F32))
        key_a[rows] = jnp.where(first, keys, 0.0).astype(BF16)
        key_b[rows] = jnp.where(first, 0.0, keys).astype(BF16)
        value_t[0:PAIR, rows] = kv[PAIR : 2 * PAIR]

    place(send_kv[3, x], me)
    recv_q[me] = send_q[3, x]

    def source(n):
        i = n // 4
        off = jnp.where(i == 0, 2, jnp.where(i == 1, 3, jnp.where(i == 2, 1, 0)))
        return lax.rem(zh + off, 4) * 4 + lax.rem(x + 1 + lax.rem(n, 4), 4)

    def arrive(n, carry):
        j = source(n)
        pltpu.make_async_remote_copy(
            src_ref=send_kv.at[0, 0], dst_ref=recv_kv.at[j], send_sem=kv_ssem.at[0, 0],
            recv_sem=kv_rsem.at[j], device_id={"space": j}, device_id_type=MESH,
        ).wait_recv()
        place(recv_kv[j], j)
        return carry

    lax.fori_loop(0, SPACE - 1, arrive, 0)

    def wait_q(n, carry):
        j = source(n)
        pltpu.make_async_remote_copy(
            src_ref=send_q.at[0, 0], dst_ref=recv_q.at[j], send_sem=q_ssem.at[0, 0],
            recv_sem=q_rsem.at[j], device_id={"space": j}, device_id_type=MESH,
        ).wait_recv()
        return carry

    lax.fori_loop(0, SPACE - 1, wait_q, 0)

    factor = math.log2(math.e) / math.sqrt(HD)
    row = lax.broadcasted_iota(jnp.int32, (PAIR, 2 * PATCHES), 0)

    def o_copy(j):
        return pltpu.make_async_remote_copy(
            src_ref=send_o.at[j],
            dst_ref=out.at[me],
            send_sem=o_ssem.at[j],
            recv_sem=o_rsem.at[me],
            device_id={"space": j},
            device_id_type=MESH,
        )

    def attend(n, carry):
        b = lax.rem(me // 2 + 1 + n, SPACE // 2)
        queries = jnp.concatenate([recv_q[2 * b], recv_q[2 * b + 1]], axis=1)
        mixed = []
        for keys in (key_a, key_b):
            scores = jnp.dot(keys[...], queries, preferred_element_type=F32)
            top = jnp.max(scores, axis=0, keepdims=True)
            weights = jnp.exp2((scores - top) * factor).astype(BF16)
            both = jnp.dot(value_t[...], weights, preferred_element_type=F32)
            mixed.append(both[0:PAIR] / both[PAIR : PAIR + 1])
        result = jnp.where(row < HD, mixed[0], mixed[1]).astype(BF16)
        for e in range(2):
            j = 2 * b + e
            send_o[j] = result[:, e * PATCHES : (e + 1) * PATCHES]

            @pl.when(j != me)
            def _():
                o_copy(j).start()

        return carry

    lax.fori_loop(0, SPACE // 2, attend, 0)
    own = pltpu.make_async_copy(send_o.at[me], out.at[me], local_sem)
    own.start()
    own.wait()

    for i, k in remote:
        copy_to(i, k, send_kv, recv_kv, kv_ssem, kv_rsem).wait_send()
        copy_to(i, k, send_q, recv_q, q_ssem, q_rsem).wait_send()

    def finish(n, carry):
        j = lax.rem(me + 1 + n, SPACE)
        o_copy(j).wait_send()
        pltpu.make_async_remote_copy(
            src_ref=send_o.at[j], dst_ref=out.at[j], send_sem=o_ssem.at[j],
            recv_sem=o_rsem.at[j], device_id={"space": j}, device_id_type=MESH,
        ).wait_recv()
        return carry

    lax.fori_loop(0, SPACE - 1, finish, 0)


def space_attention(video, pos, table, shift, scale, w):
    vmem = pl.BlockSpec(memory_space=pltpu.VMEM)
    dma = pltpu.SemaphoreType.DMA
    tokens = SPACE * PATCHES
    return pl.pallas_call(
        space_kernel,
        out_shape=jax.ShapeDtypeStruct((SPACE, PAIR, PATCHES), BF16),
        in_specs=[vmem] * 5 + [pl.BlockSpec(memory_space=pl.ANY)],
        out_specs=vmem,
        scratch_shapes=[
            pltpu.VMEM((4, 4, 2 * PAIR, PATCHES), BF16),
            pltpu.VMEM((4, 4, PAIR, PATCHES), BF16),
            pltpu.VMEM((SPACE, 2 * PAIR, PATCHES), BF16),
            pltpu.VMEM((SPACE, PAIR, PATCHES), BF16),
            pltpu.VMEM((SPACE, PAIR, PATCHES), BF16),
            pltpu.VMEM((tokens, PAIR), BF16),
            pltpu.VMEM((tokens, PAIR), BF16),
            pltpu.VMEM((PAIR + 16, tokens), BF16),
            pltpu.VMEM((3 * INNER, D), BF16),
            dma((4, 4)), dma((SPACE,)), dma((4, 4)), dma((SPACE,)), dma((SPACE,)), dma((SPACE,)), dma, dma((3,)),
        ],
        compiler_params=pltpu.CompilerParams(
            collective_id=1, has_side_effects=True, vmem_limit_bytes=52 * 2**20
        ),
        name="space_attention",
    )(video, pos, table, shift, scale, w)


def time_kernel(
    attended, video, frame_pos, table, gate_s, out_s, shift, scale, gate_t, w, out_t, out,
    w_held, out_held, after, send, recv, total, send_o, recv_o,
    ssem, rsem, o_ssem, o_rsem, w_sem,
):
    me = lax.axis_index("tm")

    loads = []
    for n, (here, there) in enumerate(((0, 0), (2, 1), (1, 2))):
        loads.append(
            pltpu.make_async_copy(
                w.at[pl.ds(here * INNER, INNER)], w_held.at[pl.ds(there * INNER, INNER)], w_sem.at[n]
            )
        )
    loads.append(pltpu.make_async_copy(out_t, out_held.at[pl.ds(HALF, INNER)], w_sem.at[3]))
    for load in loads:
        load.start()
    w_held[3 * INNER :] = jnp.zeros((HALF, D), BF16)
    out_held[0:HALF] = jnp.zeros((HALF, D), BF16)

    barrier = pltpu.get_barrier_semaphore()
    for k in range(1, TM):
        other = lax.rem(me + k, TM)
        pl.semaphore_signal(barrier, 1, device_id={"tm": other}, device_id_type=MESH)

    angles = frame_pos[:, 0:1] * table[0:1, :]
    cosine = jnp.cos(angles)
    sine = jnp.sin(angles)
    lead = sine * table[1:2, :]
    trail = sine * table[2:3, :]

    def send_copy(i, k):
        d = lax.rem(me + k, TM)
        return pltpu.make_async_remote_copy(
            src_ref=send.at[i, d], dst_ref=recv.at[i, me], send_sem=ssem.at[i, d],
            recv_sem=rsem.at[i, me], device_id={"tm": d}, device_id_type=MESH,
        )

    for i in range(2):
        mixed = jnp.concatenate(
            [jnp.transpose(attended[2 * i + e].astype(F32)).astype(BF16) for e in range(2)], axis=0
        )
        branch = jnp.dot(mixed, out_s[...], preferred_element_type=F32)
        stream = video[2 * i : 2 * i + 2].reshape(2 * PATCHES, D).astype(F32)
        stream = (stream + gate_s[...] * branch).astype(BF16)
        after[2 * i : 2 * i + 2] = stream.reshape(2, PATCHES, D)
        modulated = (normalize(stream) * (1.0 + scale[...]) + shift[...]).astype(BF16)
        if i == 0:
            for load in loads[:3]:
                load.wait()
        y = lax.dot_general(
            modulated, w_held[...], (((1,), (1,)), ((), ())), preferred_element_type=F32
        )
        sides = []
        for e in range(2):
            f = 2 * i + e
            rows = y[e * PATCHES : (e + 1) * PATCHES]
            angle = (cosine[f : f + 1], lead[f : f + 1], trail[f : f + 1])
            side = jnp.concatenate(
                [
                    rotated(rows[:, 0:WIDE], *angle, HD // 2, 1),
                    rows[:, WIDE : 2 * INNER],
                    rotated(rows[:, 2 * INNER :], *angle, HD // 2, 1),
                ],
                axis=1,
            )
            sides.append(side.reshape(TM, 8, LANES))
        send[i] = jnp.stack(sides, axis=1).reshape(TM, 16, LANES).astype(BF16)
        if i == 0:
            pl.semaphore_wait(barrier, TM - 1)
        for k in range(1, TM):
            send_copy(i, k).start()
        recv[i, me] = send[i, me]

    def wait_rows(k, carry):
        j = lax.rem(me + k, TM)
        for i in range(2):
            pltpu.make_async_remote_copy(
                src_ref=send.at[i, j], dst_ref=recv.at[i, j], send_sem=ssem.at[i, j],
                recv_sem=rsem.at[i, j], device_id={"tm": j}, device_id_type=MESH,
            ).wait_recv()
        return carry

    lax.fori_loop(1, TM, wait_rows, 0)

    count = 4 * TM * 8
    factor = math.log2(math.e) / math.sqrt(HD)
    same = lax.rem(lax.broadcasted_iota(jnp.int32, (count, count), 0), 8) == lax.rem(
        lax.broadcasted_iota(jnp.int32, (count, count), 1), 8
    )

    def window(start):
        low = start // 128 * 128
        high = (start + HD + 127) // 128 * 128
        lane = lax.broadcasted_iota(jnp.int32, (count, high - low), 1)
        return low, high, (lane >= start - low) & (lane < start - low + HD)

    total[...] = jnp.zeros((count, WIDE), F32)
    for h in range(HEADS):
        low, high, inside = window(h * HD)
        queries = recv[:, :, :, low:high].reshape(count, high - low)
        keys = recv[:, :, :, 2 * INNER + low : 2 * INNER + high].reshape(count, high - low)
        keys = jnp.where(inside, keys, jnp.zeros_like(keys))
        scores = lax.dot_general(
            queries, keys, (((1,), (1,)), ((), ())), preferred_element_type=F32
        )
        scores = jnp.where(same, scores, -1e30)
        top = jnp.max(scores, axis=1, keepdims=True)
        weights = jnp.exp2((scores - top) * factor)
        sums = jnp.sum(weights, axis=1, keepdims=True)
        low, high, inside = window(HALF + h * HD)
        base = INNER - HALF
        values = recv[:, :, :, base + low : base + high].reshape(count, high - low)
        part = jnp.dot(weights.astype(BF16), values, preferred_element_type=F32)
        total[:, low:high] += jnp.where(inside, part / sums, 0.0)
    send_o[...] = total[...].astype(BF16).reshape(2, TM, 16, WIDE)

    def o_copy(k):
        d = lax.rem(me + k, TM)
        return pltpu.make_async_remote_copy(
            src_ref=send_o.at[:, d], dst_ref=recv_o.at[:, me], send_sem=o_ssem.at[d],
            recv_sem=o_rsem.at[me], device_id={"tm": d}, device_id_type=MESH,
        )

    for k in range(1, TM):
        o_copy(k).start()
    recv_o[:, me] = send_o[:, me]

    def wait_o(k, carry):
        j = lax.rem(me + k, TM)
        pltpu.make_async_remote_copy(
            src_ref=send_o.at[:, j], dst_ref=recv_o.at[:, j], send_sem=o_ssem.at[j],
            recv_sem=o_rsem.at[j], device_id={"tm": j}, device_id_type=MESH,
        ).wait_recv()
        return carry

    lax.fori_loop(1, TM, wait_o, 0)
    loads[3].wait()
    for i in range(2):
        branch = jnp.dot(
            recv_o[i].reshape(2 * PATCHES, WIDE), out_held[...], preferred_element_type=F32
        ).reshape(TM, 2, 8, D)
        for e in range(2):
            f = 2 * i + e
            part = branch[:, e].reshape(PATCHES, D)
            out[f] = (after[f].astype(F32) + gate_t[...] * part).astype(BF16)

    def wait_sends(k, carry):
        d = lax.rem(me + k, TM)
        for i in range(2):
            pltpu.make_async_remote_copy(
                src_ref=send.at[i, d], dst_ref=recv.at[i, me], send_sem=ssem.at[i, d],
                recv_sem=rsem.at[i, me], device_id={"tm": d}, device_id_type=MESH,
            ).wait_send()
        o_copy(k).wait_send()
        return carry

    lax.fori_loop(1, TM, wait_sends, 0)


def time_attention(attended, video, frame_pos, table, gate_s, out_s, shift, scale, gate_t, w, out_t):
    vmem = pl.BlockSpec(memory_space=pltpu.VMEM)
    hbm = pl.BlockSpec(memory_space=pl.ANY)
    dma = pltpu.SemaphoreType.DMA
    return pl.pallas_call(
        time_kernel,
        out_shape=jax.ShapeDtypeStruct((FRAMES, PATCHES, D), BF16),
        in_specs=[vmem] * 9 + [hbm] * 2,
        out_specs=vmem,
        scratch_shapes=[
            pltpu.VMEM((LANES, D), BF16),
            pltpu.VMEM((WIDE, D), BF16),
            pltpu.VMEM((FRAMES, PATCHES, D), BF16),
            pltpu.VMEM((2, TM, 16, LANES), BF16),
            pltpu.VMEM((2, TM, 16, LANES), BF16),
            pltpu.VMEM((4 * TM * 8, WIDE), F32),
            pltpu.VMEM((2, TM, 16, WIDE), BF16),
            pltpu.VMEM((2, TM, 16, WIDE), BF16),
            dma((2, TM)), dma((2, TM)), dma((TM,)), dma((TM,)), dma((4,)),
        ],
        compiler_params=pltpu.CompilerParams(
            collective_id=2, has_side_effects=True, vmem_limit_bytes=52 * 2**20
        ),
        name="time_attention",
    )(attended, video, frame_pos, table, gate_s, out_s, shift, scale, gate_t, w, out_t)


def space_table():
    f = 10000.0 ** (-np.arange(HD // 4, dtype=np.float32) / (HD // 4))
    zero = np.zeros_like(f)
    one = np.ones_like(f)
    table = np.zeros((HD, 8), np.float32)
    table[:, 0] = np.concatenate([f, f, zero, zero])
    table[:, 1] = np.concatenate([zero, zero, f, f])
    table[:, 2] = np.concatenate([-one, zero, -one, zero])
    table[:, 3] = np.concatenate([zero, one, zero, one])
    return jnp.asarray(table)


def time_table():
    f = 10000.0 ** (-np.arange(HD // 2, dtype=np.float32) / (HD // 2))
    zero = np.zeros_like(f)
    one = np.ones_like(f)
    table = np.zeros((8, WIDE), np.float32)
    table[0, :INNER] = np.tile(np.concatenate([f, f]), HEADS)
    table[1, :INNER] = np.tile(np.concatenate([-one, zero]), HEADS)
    table[2, :INNER] = np.tile(np.concatenate([zero, one]), HEADS)
    return jnp.asarray(table)


def body(
    video,
    row_index,
    col_index,
    frame_index,
    spatial_shift,
    spatial_scale,
    spatial_gate,
    spatial_qkv,
    spatial_out,
    temporal_shift,
    temporal_scale,
    temporal_gate,
    temporal_qkv,
    temporal_out,
):
    pos = jnp.stack([row_index, col_index], axis=0).astype(F32)
    attended = space_attention(
        video, pos, space_table(), spatial_shift[None], spatial_scale[None], spatial_qkv.T
    )
    return time_attention(
        attended.reshape(FRAMES, INNER, PATCHES),
        video,
        frame_index.astype(F32)[:, None],
        time_table(),
        spatial_gate[None],
        spatial_out,
        temporal_shift[None],
        temporal_scale[None],
        temporal_gate[None],
        temporal_qkv.T,
        temporal_out,
    )


def solution(mesh):
    return jax.shard_map(
        body,
        mesh=mesh,
        in_specs=(P("tm", "space", None), P("space"), P("space"), P("tm")) + (P(),) * 10,
        out_specs=P("tm", "space", None),
        check_vma=False,
    )
```

time: 195 us -> 132 us (0.68); the launches traced: 191 us -> 132 us
  Pallas kernels: 78.8 us -> 123 us
  waiting for transfers between devices: 37 us -> 0 us
  blocking collectives: 18.8 us -> 0 us
  local copies, waits for them, and re-layouts: 25.4 us -> 7.35 us
  starting transfers between devices: 14.8 us -> 0 us
  matrix products: 9.68 us -> 0 us
  other arithmetic: 6.81 us -> 1.34 us
    pallas_call x0 -> x1, Pallas kernels: none -> 46.4 us  [time_attention(): pl.pallas_call(time_kernel, out_shape=jax.ShapeDtypeStruct((FRAMES, PATCH...]
    all_to_all x3 -> x0, waiting for transfers between devices: 37 us -> none  [the longest x1 12.9 us: body(): lax.all_to_all(time_queries, 'tm', split_axis=1, concat_axis=0, tiled=True)]
    all_to_all x1 -> x0, blocking collectives: 18.8 us -> none  [body(): lax.all_to_all(time_mixed, 'tm', split_axis=0, concat_axis=1, tiled=True)]
    all_to_all x3 -> x0, starting transfers between devices: 14.8 us -> none  [the longest x1 5.52 us: body(): lax.all_to_all(time_keys, 'tm', split_axis=1, concat_axis=0, tiled=True)]
    dot_general x5 -> x0, matrix products: 9.68 us -> none  [the longest x2 5.04 us: residual_add(): jnp.dot(attended.reshape(frames_here * patches_here, -1), weights, prefer...]
    unnamed x23 -> x7, local copies, waits for them, and re-layouts: 9.05 us -> 3.06 us
    all_to_all x4 -> x0, local copies, waits for them, and re-layouts: 4.96 us -> none  [the longest x1 1.81 us: body(): lax.all_to_all(time_queries, 'tm', split_axis=1, concat_axis=0, tiled=True)]
    concatenate x2 -> x0, local copies, waits for them, and re-layouts: 4.29 us -> none  [rotate(): jnp.concatenate([leading * cosine - trailing * sines, trailing * cosine +...]
  transfers between devices with their start and end apart: 3 -> 0, of which waited for: 3 -> 0; matrix products, arithmetic and copies ran while one was open for 6% -> 0% of each run, Pallas kernels for 0% -> 0%
where the time goes in v2:
time: 132 us
  Pallas kernels  123 us (93%)
  local copies, waits for them, and re-layouts  7.35 us (6%)
  other arithmetic  1.34 us (1%)
    pallas_call x1, Pallas kernels, space_attention(): pl.pallas_call(space_kernel, out_shape=jax.ShapeDtypeStruct((SPACE, PAIR,...  76.5 us
    pallas_call x1, Pallas kernels, time_attention(): pl.pallas_call(time_kernel, out_shape=jax.ShapeDtypeStruct((FRAMES, PATCH...  46.4 us
    unnamed x7, local copies, waits for them, and re-layouts  3.06 us

profile of v2, /device:TPU:1, one launch (start us, length us, event | category | flops | bytes accessed | tf_op | source)
XLA Modules:
  0.0 131.7 jit_solution(17907262292177043846)
XLA Ops:
  0.0 0.7 convert_bitcast_fusion
  0.7 0.7 add_convert_fusion.pos
  1.3 0.1 copy.17.frame_pos
  1.4 0.7 broadcast_in_dim.21.shift
  2.1 0.7 broadcast_in_dim.22.scale
  2.8 0.7 broadcast_in_dim.24.gate_s
  3.5 0.7 broadcast_in_dim.25.shift
  4.2 0.7 broadcast_in_dim.26.scale
  4.9 0.7 broadcast_in_dim.27.gate_t
  5.6 0.0 copy-start
  5.6 1.3 copy-done
  6.9 0.0 copy-start.1
  6.9 0.8 copy-done.1
  7.7 0.0 copy-start.2
  7.7 76.5 %space_attention.1 = bf16[16,144,128]{2,1,0:T(8,128)(2,1)S(1)} custom-call(bf16[4,128,1152]{2,1,0:T(8,128)(2,1)S(1)} %copy-done, f32[2,128]{1,0:T(2,128)S(1)} %add_convert_fusion.pos, f32[72,8]{1,0:T(8,128)S(1)} %copy-done.1, f32[1,1152]{1,0:T(1,128)S(1)} %broadcast_in_dim.21.shift, f32[1,1152]{1,0:T(1,128)S(1)} %broadcast_in_dim.22.scale, ...), custom_call_target="tpu_custom_call" | custom-call | tf_op jit(solution)/shard_map/space_attention/pallas_call | solution.py:226
  84.2 0.0 copy-done.2
  84.2 46.4 %time_attention.1 = bf16[4,128,1152]{2,1,0:T(8,128)(2,1)S(1)} custom-call(bf16[4,576,128]{2,1,0:T(8,128)(2,1)S(1)} %bitcast.7, bf16[4,128,1152]{2,1,0:T(8,128)(2,1)} %video.3, f32[4,1]{1,0:T(4,128)S(1)} %copy.17.frame_pos, f32[8,640]{1,0:T(8,128)S(1)} %copy-done.2, f32[1,1152]{1,0:T(1,128)S(1)} %broadcast_in_dim.24.gate_s, bf16[576,1152]{1,0:T(8,128)(2,1)} %out_s.1, ...), custom_call_target="tpu_custom_call" | custom-call | tf_op jit(solution)/shard_map/time_attention/pallas_call | solution.py:414
  130.7 1.0 copy.19
Async XLA Ops:
  5.6 1.3 copy-start
  6.9 0.8 copy-start.1
  7.7 76.5 %copy-start.2 = (f32[8,640]{1,0:T(8,128)S(1)}, f32[8,640]{1,0:T(8,128)}, u32[]{:S(2)}) copy-start(f32[8,640]{1,0:T(8,128)} %constant.5.clone.table) | copy-start | bytes 61444

commit v3 on v0

v3 whole, which is shorter than its diff:
```python
import math

import jax
import jax.numpy as jnp
import numpy as np
from jax import lax
from jax.experimental import pallas as pl
from jax.experimental.pallas import tpu as pltpu
from jax.sharding import PartitionSpec as P

HEADS = 8
HD = 72
D = 1152
INNER = HEADS * HD
FRAMES = 4
PATCHES = 128
SPACE = 16
PAIR = 2 * HD
TM = 16
NEAR = 8
TOKENS = FRAMES * PATCHES
KEYS = SPACE * PATCHES
HALF = INNER % 128
WIDE = INNER + HALF
LANES = 3 * INNER + HALF
FACTOR = math.log2(math.e) / math.sqrt(HD)
CHUNK = 512
EPSILON = 1e-06
MESH = pl.DeviceIdType.MESH
BF16 = jnp.bfloat16
F32 = jnp.float32


def modulated(stream, scale, shift):
    stream = stream.astype(F32)
    centre = stream - jnp.mean(stream, axis=-1, keepdims=True)
    spread = jnp.mean(centre * centre, axis=-1, keepdims=True)
    normal = centre * lax.rsqrt(spread + EPSILON)
    return (normal * (1.0 + scale) + shift).astype(BF16)


def rotated(u, cosine, lead, trail, half, axis):
    ahead = pltpu.roll(u, u.shape[axis] - half, axis)
    behind = pltpu.roll(u, half, axis)
    return u * cosine + ahead * lead + behind * trail


def matmul(a, b):
    return jnp.dot(a, b, preferred_element_type=F32)


def matmul_t(a, b):
    return lax.dot_general(a, b, (((1,), (1,)), ((), ())), preferred_element_type=F32)


def kernel(
    video, row_index, col_index, frame_index,
    shift_s, scale_s, gate_s, w_s, out_s, shift_t, scale_t, gate_t, w_t, out_t, table_s, table_t,
    out,
    video_held, w_s_held, out_s_held, w_t_held, out_t_held,
    pos, z_recv, pos_recv, frame_recv, frame_rows, time_rows, time_tables,
    x_send, x_recv, key_a, key_b, value_t, score_a, score_b, o_send, o_recv,
    t_send, t_recv, joined, total, r_send, r_recv,
    l_sem, z_ssem, z_rsem, p_ssem, p_rsem, f_ssem, f_rsem, x_ssem, x_rsem,
    o_ssem, o_rsem, t_ssem, t_rsem, r_ssem, r_rsem,
):
    tm = lax.axis_index("tm")
    space = lax.axis_index("space")
    zh = space // 4
    x = lax.rem(space, 4)
    zl = tm // NEAR
    yc = lax.rem(tm, NEAR)

    def remote(src, dst, ssem, rsem, **device):
        return pltpu.make_async_remote_copy(
            src_ref=src, dst_ref=dst, send_sem=ssem, recv_sem=rsem, device_id=device, device_id_type=MESH
        )

    barrier = pltpu.get_barrier_semaphore()
    for k in range(1, SPACE):
        other = {"space": lax.rem(space + k, SPACE)}
        pl.semaphore_signal(barrier, 1, device_id=other, device_id_type=MESH)
    for k in range(1, TM):
        other = {"tm": lax.rem(tm + k, TM)}
        pl.semaphore_signal(barrier, 1, device_id=other, device_id_type=MESH)

    def load(n, src, dst):
        copy = pltpu.make_async_copy(src, dst, l_sem.at[n])
        copy.start()
        return copy

    load_own = load(0, video.at[zh], video_held.at[zh])
    load_w_s = load(1, w_s, w_s_held)
    load_rest = [
        load(1 + k, video.at[lax.rem(zh + k, 4)], video_held.at[lax.rem(zh + k, 4)])
        for k in range(1, 4)
    ]
    load_out_s = load(5, out_s, out_s_held)
    load_w_t = [
        load(6 + n, w_t.at[pl.ds(here * INNER, INNER)], w_t_held.at[pl.ds(there * INNER, INNER)])
        for n, (here, there) in enumerate(((0, 0), (2, 1), (1, 2)))
    ]
    load_out_t = load(9, out_t, out_t_held.at[pl.ds(HALF, INNER)])

    row = lax.broadcasted_iota(jnp.int32, (8, PATCHES), 0)
    here = jnp.where(
        row == 0, row_index[...].reshape(1, PATCHES), col_index[...].reshape(1, PATCHES)
    )
    pos[...] = here.astype(F32)
    times = jnp.zeros((8, 128), jnp.int32)
    for f in range(FRAMES):
        times = jnp.where(row == f, frame_index[f], times)
    frame_recv[tm] = times.astype(F32)

    def z_copy(n):
        f = lax.rem(zh + (1, 3, 2)[n], 4)
        to = {"space": f * 4 + x}
        slot = (1, 0, 2)[n]
        return (
            remote(video.at[f], z_recv.at[slot], z_ssem.at[n], z_rsem.at[slot], **to),
            remote(pos, pos_recv.at[slot], p_ssem.at[n], p_rsem.at[slot], **to),
        )

    def frame_copy(k):
        d = lax.rem(tm + k, TM)
        return remote(
            frame_recv.at[tm], frame_recv.at[tm], f_ssem.at[d], f_rsem.at[tm], tm=d
        )

    pl.semaphore_wait(barrier, SPACE + TM - 2)
    for n in range(3):
        for copy in z_copy(n):
            copy.start()
    for k in range(1, TM):
        frame_copy(k).start()

    offsets = (0, 1, 3, 2)

    def block(c, column):
        return lax.rem(zh + offsets[c], 4) * 4 + column

    def x_copy(c, k):
        d = lax.rem(x + k, 4)
        mine = block(c, x)
        return remote(
            x_send.at[c, d], x_recv.at[mine], x_ssem.at[c, k], x_rsem.at[mine], space=zh * 4 + d
        )

    head_row = lax.broadcasted_iota(jnp.int32, (PATCHES, PAIR), 1) < HD

    def place(c, column, held):
        b = block(c, column)
        rows = pl.ds(pl.multiple_of(b * PATCHES, PATCHES), PATCHES)
        keys = jnp.transpose(held[PAIR : 2 * PAIR].astype(F32))
        key_a[rows] = jnp.where(head_row, keys, 0.0).astype(BF16)
        key_b[rows] = jnp.where(head_row, 0.0, keys).astype(BF16)
        value_t[0:PAIR, rows] = held[2 * PAIR :]

    def project(first, streams, places):
        y = matmul_t(
            w_s_held[...],
            jnp.concatenate(
                [modulated(s, scale_s[...].reshape(1, D), shift_s[...].reshape(1, D)) for s in streams],
                axis=0,
            ),
        )
        for e, at in enumerate(places):
            angles = table_s[:, 0:1] * at[0:1, :] + table_s[:, 1:2] * at[1:2, :]
            cosine = jnp.cos(angles)
            sine = jnp.sin(angles)
            lead = sine * table_s[:, 2:3]
            trail = sine * table_s[:, 3:4]
            part = y[:, e * PATCHES : (e + 1) * PATCHES]

            def turned(n):
                return rotated(part[n * HD : (n + 1) * HD], cosine, lead, trail, HD // 4, 0)

            for d in range(4):
                for n in range(2):
                    base = n * HEADS + 2 * d
                    x_send[first + e, d, n * PAIR : (n + 1) * PAIR] = jnp.concatenate(
                        [turned(base), turned(base + 1)], axis=0
                    ).astype(BF16)
                rows = slice(2 * INNER + d * PAIR, 2 * INNER + (d + 1) * PAIR)
                x_send[first + e, d, 2 * PAIR :] = part[rows].astype(BF16)
        for e in range(len(streams)):
            for k in (1, 3, 2):
                x_copy(first + e, k).start()
        for e in range(len(streams)):
            c = first + e
            place(c, x, x_send[c, x])
            x_recv[block(c, x), 0:PAIR] = x_send[c, x, 0:PAIR]

    def gather(c):
        for k in (1, 3, 2):
            column = lax.rem(x + k, 4)
            b = block(c, column)
            remote(x_send.at[c, k], x_recv.at[b], x_ssem.at[c, k], x_rsem.at[b], space=b).wait_recv()
            place(c, column, x_recv[b])

    def z_arrived(slot):
        f = lax.rem(zh + (1, 3, 2)[slot], 4)
        to = {"space": f * 4 + x}
        remote(video.at[f], z_recv.at[slot], z_ssem.at[slot], z_rsem.at[slot], **to).wait_recv()
        remote(pos, pos_recv.at[slot], p_ssem.at[slot], p_rsem.at[slot], **to).wait_recv()

    load_own.wait()
    load_w_s.wait()
    project(0, [video_held[zh]], [pos[...]])

    w_t_held[3 * INNER :] = jnp.zeros((HALF, D), BF16)
    out_t_held[0:HALF] = jnp.zeros((HALF, D), BF16)
    value_t[PAIR:] = jnp.where(
        lax.broadcasted_iota(jnp.int32, (16, KEYS), 0) == 0, 1.0, 0.0
    ).astype(BF16)

    def frame_arrived(k, carry):
        j = lax.rem(tm + k, TM)
        remote(frame_recv.at[tm], frame_recv.at[j], f_ssem.at[j], f_rsem.at[j], tm=j).wait_recv()
        return carry

    lax.fori_loop(1, TM, frame_arrived, 0)

    def side(s):
        return lax.rem(zl + s, 2) * NEAR

    for s in range(2):
        for n in range(NEAR):
            for i in range(2):
                at = s * 32 + i * 16 + n * 2
                frame_rows[at : at + 2] = frame_recv[side(s) + n, 2 * i : 2 * i + 2]
    angles = frame_rows[:, 0:1] * table_t[0:1, :]
    sine = jnp.sin(angles)
    time_rows[0] = jnp.cos(angles)
    time_rows[1] = sine * table_t[1:2, :]
    time_rows[2] = sine * table_t[2:3, :]

    def widen(g, carry):
        rows = pl.ds(pl.multiple_of(g * 8, 8), 8)
        for n in range(3):
            time_tables[n, rows] = jnp.broadcast_to(time_rows[n, pl.ds(g, 1)], (8, WIDE))
        return carry

    lax.fori_loop(0, 64, widen, 0)

    gather(0)
    z_arrived(0)
    z_arrived(1)
    project(1, [z_recv[0], z_recv[1]], [pos_recv[0], pos_recv[1]])
    gather(1)
    gather(2)
    z_arrived(2)
    project(3, [z_recv[2]], [pos_recv[2]])
    gather(3)

    def o_copy(j):
        return remote(o_send.at[j], o_recv.at[space], o_ssem.at[j], o_rsem.at[space], space=j)

    pair_row = lax.broadcasted_iota(jnp.int32, (PAIR, 2 * PATCHES), 0) < HD
    chunks = [slice(n * CHUNK, (n + 1) * CHUNK) for n in range(KEYS // CHUNK)]

    def attend(n, carry):
        b = lax.rem(space // 2 + 1 + n, SPACE // 2)
        queries = jnp.concatenate([x_recv[2 * b, 0:PAIR], x_recv[2 * b + 1, 0:PAIR]], axis=1)
        tops = []
        for keys, scores in ((key_a, score_a), (key_b, score_b)):
            top = None
            for rows in chunks:
                product = matmul(keys[rows], queries)
                scores[rows] = product
                high = jnp.max(product.reshape(CHUNK // 8, 8, 2 * PATCHES), axis=0)
                top = high if top is None else jnp.maximum(top, high)
            tops.append(jnp.max(top, axis=0, keepdims=True))
        mixed = []
        for scores, top in zip((score_a, score_b), tops):
            both = None
            for rows in chunks:
                weights = jnp.exp2((scores[rows] - top) * FACTOR).astype(BF16)
                product = matmul(value_t[:, rows], weights)
                both = product if both is None else both + product
            mixed.append(both[0:PAIR] / both[PAIR : PAIR + 1])
        result = jnp.where(pair_row, mixed[0], mixed[1]).astype(BF16)
        for e in range(2):
            j = 2 * b + e
            o_send[j] = result[:, e * PATCHES : (e + 1) * PATCHES]

            @pl.when(j != space)
            def _():
                o_copy(j).start()

        return carry

    lax.fori_loop(0, SPACE // 2, attend, 0)
    o_recv[space] = o_send[space]

    def t_copy(i, d):
        return remote(t_send.at[i, d], t_recv.at[i, tm], t_ssem.at[i, d], t_rsem.at[i, tm], tm=d)

    peers = [(s, r) for s in (1, 0) for r in range(NEAR) if (s, r) != (0, 0)]

    def peer(s, r):
        return side(s) + lax.rem(yc + r, NEAR)

    for copy in load_rest:
        copy.wait()
    load_out_s.wait()
    for i in range(2):

        def o_arrived(n, carry):
            j = i * 8 + n

            @pl.when(j != space)
            def _():
                remote(o_send.at[j], o_recv.at[j], o_ssem.at[j], o_rsem.at[j], space=j).wait_recv()

            return carry

        lax.fori_loop(0, 8, o_arrived, 0)
        mixed = []
        for e in range(2):
            f = 2 * i + e
            attended = o_recv[4 * f : 4 * f + 4].reshape(INNER, PATCHES)
            mixed.append(jnp.transpose(attended.astype(F32)).astype(BF16))
        branch = matmul(jnp.concatenate(mixed, axis=0), out_s_held[...])
        stream = video_held[2 * i : 2 * i + 2].reshape(2 * PATCHES, D).astype(F32)
        stream = (stream + gate_s[...].reshape(1, D) * branch).reshape(2, TM, 8, D)
        t_send[i] = jnp.stack([stream[0], stream[1]], axis=1).reshape(TM, 16, D).astype(BF16)
        for s, r in peers:
            t_copy(i, peer(s, r)).start()
        t_recv[i, tm] = t_send[i, tm]

    for copy in load_w_t:
        copy.wait()
    for s in range(2):
        for r in range(NEAR):
            if (s, r) != (0, 0):
                j = peer(s, r)
                for i in range(2):
                    remote(
                        t_send.at[i, j], t_recv.at[i, j], t_ssem.at[i, j], t_rsem.at[i, j], tm=j
                    ).wait_recv()
        rows = t_recv[:, pl.ds(side(s), NEAR)].reshape(2 * PATCHES, D)
        y = matmul_t(
            modulated(rows, scale_t[...].reshape(1, D), shift_t[...].reshape(1, D)), w_t_held[...]
        )
        angle = [time_tables[n, s * 256 : (s + 1) * 256] for n in range(3)]
        joined[s, :, 0:WIDE] = rotated(y[:, 0:WIDE], *angle, HD // 2, 1).astype(BF16)
        joined[s, :, WIDE : 2 * INNER] = y[:, WIDE : 2 * INNER].astype(BF16)
        joined[s, :, 2 * INNER :] = rotated(y[:, 2 * INNER :], *angle, HD // 2, 1).astype(BF16)

    def r_copy(s, r):
        d = peer(s, r)
        n = lax.rem(yc + r, NEAR)
        return remote(r_send.at[s, :, n], r_recv.at[:, tm], r_ssem.at[d], r_rsem.at[tm], tm=d)

    def window(start, count):
        low = start // 128 * 128
        high = (start + HD + 127) // 128 * 128
        lane = lax.broadcasted_iota(jnp.int32, (count, high - low), 1)
        return low, high, (lane >= start - low) & (lane < start - low + HD)

    same = lax.rem(lax.broadcasted_iota(jnp.int32, (256, TOKENS), 0), 8) == lax.rem(
        lax.broadcasted_iota(jnp.int32, (256, TOKENS), 1), 8
    )
    for s in (1, 0):
        total[...] = jnp.zeros((256, WIDE), F32)
        for h in range(HEADS):
            low, high, inside = window(h * HD, TOKENS)
            keys = joined[:, :, 2 * INNER + low : 2 * INNER + high].reshape(TOKENS, high - low)
            keys = jnp.where(inside, keys, jnp.zeros_like(keys))
            scores = jnp.where(same, matmul_t(joined[s, :, low:high], keys), -1e30)
            top = jnp.max(scores, axis=1, keepdims=True)
            weights = jnp.exp2((scores - top) * FACTOR)
            sums = jnp.sum(weights, axis=1, keepdims=True)
            low, high, inside = window(HALF + h * HD, 256)
            base = INNER - HALF
            values = joined[:, :, base + low : base + high].reshape(TOKENS, high - low)
            part = matmul(weights.astype(BF16), values)
            total[:, low:high] += jnp.where(inside, part / sums, 0.0)
        r_send[s] = total[...].astype(BF16).reshape(2, NEAR, 16, WIDE)
        for r in range(NEAR):
            if (s, r) != (0, 0):
                r_copy(s, r).start()
    r_recv[:, tm] = r_send[0, :, yc]

    def r_arrived(k, carry):
        j = lax.rem(tm + k, TM)
        remote(r_send.at[0, :, 0], r_recv.at[:, j], r_ssem.at[j], r_rsem.at[j], tm=j).wait_recv()
        return carry

    lax.fori_loop(1, TM, r_arrived, 0)
    load_out_t.wait()
    for i in range(2):
        branch = matmul(r_recv[i].reshape(2 * PATCHES, WIDE), out_t_held[...])
        stream = t_send[i].reshape(2 * PATCHES, D).astype(F32)
        stream = (stream + gate_t[...].reshape(1, D) * branch).reshape(TM, 2, 8, D)
        for e in range(2):
            out[2 * i + e] = stream[:, e].reshape(PATCHES, D).astype(BF16)

    for n in range(3):
        for copy in z_copy(n):
            copy.wait_send()
        for c in range(4):
            x_copy(c, n + 1).wait_send()

    def o_sent(k, carry):
        o_copy(lax.rem(space + k, SPACE)).wait_send()
        frame_copy(k).wait_send()
        return carry

    lax.fori_loop(1, SPACE, o_sent, 0)
    for s, r in peers:
        for i in range(2):
            t_copy(i, peer(s, r)).wait_send()
        r_copy(s, r).wait_send()


def block(*arrays):
    vmem = pl.BlockSpec(memory_space=pltpu.VMEM)
    smem = pl.BlockSpec(memory_space=pltpu.SMEM)
    hbm = pl.BlockSpec(memory_space=pl.ANY)
    dma = pltpu.SemaphoreType.DMA
    specs = [hbm, vmem, vmem, smem] + [vmem, vmem, vmem, hbm, hbm] * 2 + [vmem, vmem]
    held = [
        ((FRAMES, PATCHES, D), BF16),
        ((3 * INNER, D), BF16),
        ((INNER, D), BF16),
        ((LANES, D), BF16),
        ((WIDE, D), BF16),
        ((8, PATCHES), F32),
        ((3, PATCHES, D), BF16),
        ((3, 8, PATCHES), F32),
        ((TM, 8, 128), F32),
        ((64, 128), F32),
        ((3, 64, WIDE), F32),
        ((3, TOKENS, WIDE), F32),
        ((4, 4, 3 * PAIR, PATCHES), BF16),
        ((SPACE, 3 * PAIR, PATCHES), BF16),
        ((KEYS, PAIR), BF16),
        ((KEYS, PAIR), BF16),
        ((PAIR + 16, KEYS), BF16),
        ((KEYS, 2 * PATCHES), F32),
        ((KEYS, 2 * PATCHES), F32),
        ((SPACE, PAIR, PATCHES), BF16),
        ((SPACE, PAIR, PATCHES), BF16),
        ((2, TM, 16, D), BF16),
        ((2, TM, 16, D), BF16),
        ((2, 256, LANES), BF16),
        ((256, WIDE), F32),
        ((2, 2, NEAR, 16, WIDE), BF16),
        ((2, TM, 16, WIDE), BF16),
    ]
    sems = [(10,), (3,), (3,), (3,), (3,), (TM,), (TM,), (4, 4), (SPACE,)]
    sems += [(SPACE,), (SPACE,), (2, TM), (2, TM), (TM,), (TM,)]
    return pl.pallas_call(
        kernel,
        out_shape=jax.ShapeDtypeStruct((FRAMES, PATCHES, D), BF16),
        in_specs=specs,
        out_specs=vmem,
        scratch_shapes=[pltpu.VMEM(*h) for h in held] + [dma(s) for s in sems],
        compiler_params=pltpu.CompilerParams(
            collective_id=1, has_side_effects=True, vmem_limit_bytes=56 * 2**20
        ),
        name="space_time_block",
    )(*arrays)


def space_table():
    f = 10000.0 ** (-np.arange(HD // 4, dtype=np.float32) / (HD // 4))
    zero = np.zeros_like(f)
    one = np.ones_like(f)
    table = np.zeros((HD, 8), np.float32)
    table[:, 0] = np.concatenate([f, f, zero, zero])
    table[:, 1] = np.concatenate([zero, zero, f, f])
    table[:, 2] = np.concatenate([-one, zero, -one, zero])
    table[:, 3] = np.concatenate([zero, one, zero, one])
    return jnp.asarray(table)


def time_table():
    f = 10000.0 ** (-np.arange(HD // 2, dtype=np.float32) / (HD // 2))
    zero = np.zeros_like(f)
    one = np.ones_like(f)
    table = np.zeros((8, WIDE), np.float32)
    table[0, :INNER] = np.tile(np.concatenate([f, f]), HEADS)
    table[1, :INNER] = np.tile(np.concatenate([-one, zero]), HEADS)
    table[2, :INNER] = np.tile(np.concatenate([zero, one]), HEADS)
    return jnp.asarray(table)


def body(*arrays):
    arrays = list(arrays)
    for n in (7, 12):
        arrays[n] = arrays[n].T
    return block(*arrays, space_table(), time_table())


def solution(mesh):
    return jax.shard_map(
        body,
        mesh=mesh,
        in_specs=(P("tm", "space", None), P("space"), P("space"), P("tm")) + (P(),) * 10,
        out_specs=P("tm", "space", None),
        check_vma=False,
    )
```

time: 418 us -> 126 us (0.30)
  waiting for transfers between devices: 279 us -> 0 us
  Pallas kernels: 0 us -> 122 us
  matrix products: 45.6 us -> 0 us
  other arithmetic: 24.5 us -> 0 us
  local copies, waits for them, and re-layouts: 21.8 us -> 2.37 us
  blocking collectives: 18.8 us -> 0 us
  starting transfers between devices: 14.2 us -> 0 us
  between operations: 13.7 us -> 0.01 us
    all_gather x2 -> x0, waiting for transfers between devices: 242 us -> none  [the longest x1 135 us: body(): key_piece = lax.all_gather(key_vectors, 'space', axis=1, tiled=True)]
    pallas_call x0 -> x1, Pallas kernels: none -> 122 us  [block(): pl.pallas_call(kernel, out_shape=jax.ShapeDtypeStruct((FRAMES, PATCHES, D...]
    dot_general x8 -> x0, matrix products: 45.6 us -> none  [the longest x1 16 us: body(): jnp.einsum('fphe,fkhe->fhpk', queries, key_piece, preferred_element_type=...]
    all_to_all x3 -> x0, waiting for transfers between devices: 37.1 us -> none  [the longest x1 13 us: body(): lax.all_to_all(time_keys, 'tm', split_axis=1, concat_axis=0, tiled=True)]
    all_to_all x1 -> x0, blocking collectives: 18.8 us -> none  [body(): lax.all_to_all(time_mixed, 'tm', split_axis=0, concat_axis=1, tiled=True)]
    reduce_sum x5 -> x0, other arithmetic: 18.5 us -> none  [the longest x1 14.1 us: body(): run_sum = jnp.sum(weights, axis=-1)]
    all_to_all x3 -> x0, starting transfers between devices: 14 us -> none  [the longest x1 4.93 us: body(): lax.all_to_all(time_values, 'tm', split_axis=1, concat_axis=0, tiled=True)]
    convert_element_type x3 -> x0, local copies, waits for them, and re-layouts: 5.48 us -> none  [the longest x2 4.8 us: body(): time_values = joined[:, :, 2].astype(jnp.bfloat16)]
  transfers between devices with their start and end apart: 5 -> 0, of which waited for: 5 -> 0; matrix products, arithmetic and copies ran while one was open for 11% -> 0% of each run, Pallas kernels for 0% -> 0%
where the time goes in v3:
time: 126 us; the launch traced here: 124 us
  Pallas kernels  122 us (97%)
  local copies, waits for them, and re-layouts  2.37 us (2%)
    pallas_call x1, Pallas kernels, block(): pl.pallas_call(kernel, out_shape=jax.ShapeDtypeStruct((FRAMES, PATCHES, D...  122 us

profile of v3, /device:TPU:1, one launch (start us, length us, event | category | flops | bytes accessed | tf_op | source)
XLA Modules:
  0.0 124.1 jit_solution(2127654058384290992)
XLA Ops:
  0.0 121.7 %space_time_block.1 = bf16[4,128,1152]{2,1,0:T(8,128)(2,1)} custom-call(bf16[4,128,1152]{2,1,0:T(8,128)(2,1)} %video.1, s32[128]{0:T(128)} %row_index.1, s32[128]{0:T(128)} %col_index.1, s32[4]{0:T(128)} %frame_index.1, f32[1152]{0:T(1024)} %shift_s.1, f32[1152]{0:T(1024)} %scale_s.1, f32[1152]{0:T(1024)} %gate_s.1, bf16[1728,1152]{1,0:T(8,128)(2,1)} %bitcast.2, ...), custom_call_target="tpu_custom_call" | custom-call | tf_op jit(solution)/shard_map/space_time_block/pallas_call | solution.py:455
  121.7 2.4 %copy.18 = bf16[4,128,1152]{2,1,0:T(8,128)(2,1)} copy(bf16[4,128,1152]{2,1,0:T(8,128)(2,1)} %space_time_block.1) | data formatting | bytes 2359296

commit v4 on v3

--- a/solution.py
+++ b/solution.py
@@ -128,29 +128,23 @@
         )
 
     pl.semaphore_wait(barrier, SPACE + TM - 2)
+    for n in range(2):
+        z_copy(n)[0].start()
     for n in range(3):
-        for copy in z_copy(n):
-            copy.start()
+        z_copy(n)[1].start()
     for k in range(1, TM):
         frame_copy(k).start()
 
-    offsets = (0, 1, 3, 2)
-
-    def block(c, column):
-        return lax.rem(zh + offsets[c], 4) * 4 + column
-
     def x_copy(c, k):
         d = lax.rem(x + k, 4)
-        mine = block(c, x)
         return remote(
-            x_send.at[c, d], x_recv.at[mine], x_ssem.at[c, k], x_rsem.at[mine], space=zh * 4 + d
+            x_send.at[c, d], x_recv.at[c, x], x_ssem.at[c, k], x_rsem.at[c, x], space=zh * 4 + d
         )
 
     head_row = lax.broadcasted_iota(jnp.int32, (PATCHES, PAIR), 1) < HD
 
     def place(c, column, held):
-        b = block(c, column)
-        rows = pl.ds(pl.multiple_of(b * PATCHES, PATCHES), PATCHES)
+        rows = pl.ds(pl.multiple_of((c * 4 + column) * PATCHES, PATCHES), PATCHES)
         keys = jnp.transpose(held[PAIR : 2 * PAIR].astype(F32))
         key_a[rows] = jnp.where(head_row, keys, 0.0).astype(BF16)
         key_b[rows] = jnp.where(head_row, 0.0, keys).astype(BF16)
@@ -189,14 +183,16 @@
         for e in range(len(streams)):
             c = first + e
             place(c, x, x_send[c, x])
-            x_recv[block(c, x), 0:PAIR] = x_send[c, x, 0:PAIR]
+            x_recv[c, x, 0:PAIR] = x_send[c, x, 0:PAIR]
 
     def gather(c):
         for k in (1, 3, 2):
             column = lax.rem(x + k, 4)
-            b = block(c, column)
-            remote(x_send.at[c, k], x_recv.at[b], x_ssem.at[c, k], x_rsem.at[b], space=b).wait_recv()
-            place(c, column, x_recv[b])
+            remote(
+                x_send.at[c, k], x_recv.at[c, column], x_ssem.at[c, k], x_rsem.at[c, column],
+                space=zh * 4 + column,
+            ).wait_recv()
+            place(c, column, x_recv[c, column])
 
     def z_arrived(slot):
         f = lax.rem(zh + (1, 3, 2)[slot], 4)
@@ -243,6 +239,9 @@
 
     lax.fori_loop(0, 64, widen, 0)
 
+    for n in range(2):
+        z_copy(n)[0].wait_send()
+    z_copy(2)[0].start()
     gather(0)
     z_arrived(0)
     z_arrived(1)
@@ -260,8 +259,10 @@
     chunks = [slice(n * CHUNK, (n + 1) * CHUNK) for n in range(KEYS // CHUNK)]
 
     def attend(n, carry):
-        b = lax.rem(space // 2 + 1 + n, SPACE // 2)
-        queries = jnp.concatenate([x_recv[2 * b, 0:PAIR], x_recv[2 * b + 1, 0:PAIR]], axis=1)
+        c = 3 - n // 2
+        off = jnp.where(c == 3, 2, jnp.where(c == 2, 3, c))
+        first = lax.rem(n + x // 2 + 1, 2) * 2
+        queries = jnp.concatenate([x_recv[c, first, 0:PAIR], x_recv[c, first + 1, 0:PAIR]], axis=1)
         tops = []
         for keys, scores in ((key_a, score_a), (key_b, score_b)):
             top = None
@@ -281,7 +282,7 @@
             mixed.append(both[0:PAIR] / both[PAIR : PAIR + 1])
         result = jnp.where(pair_row, mixed[0], mixed[1]).astype(BF16)
         for e in range(2):
-            j = 2 * b + e
+            j = lax.rem(zh + off, 4) * 4 + first + e
             o_send[j] = result[:, e * PATCHES : (e + 1) * PATCHES]
 
             @pl.when(j != space)
@@ -397,9 +398,9 @@
         for e in range(2):
             out[2 * i + e] = stream[:, e].reshape(PATCHES, D).astype(BF16)
 
+    z_copy(2)[0].wait_send()
     for n in range(3):
-        for copy in z_copy(n):
-            copy.wait_send()
+        z_copy(n)[1].wait_send()
         for c in range(4):
             x_copy(c, n + 1).wait_send()
 
@@ -435,7 +436,7 @@
         ((3, 64, WIDE), F32),
         ((3, TOKENS, WIDE), F32),
         ((4, 4, 3 * PAIR, PATCHES), BF16),
-        ((SPACE, 3 * PAIR, PATCHES), BF16),
+        ((4, 4, 3 * PAIR, PATCHES), BF16),
         ((KEYS, PAIR), BF16),
         ((KEYS, PAIR), BF16),
         ((PAIR + 16, KEYS), BF16),
@@ -450,7 +451,7 @@
         ((2, 2, NEAR, 16, WIDE), BF16),
         ((2, TM, 16, WIDE), BF16),
     ]
-    sems = [(10,), (3,), (3,), (3,), (3,), (TM,), (TM,), (4, 4), (SPACE,)]
+    sems = [(10,), (3,), (3,), (3,), (3,), (TM,), (TM,), (4, 4), (4, 4)]
     sems += [(SPACE,), (SPACE,), (2, TM), (2, TM), (TM,), (TM,)]
     return pl.pallas_call(
         kernel,

time: 126 us -> 112 us (0.89); the launches traced: 124 us -> 112 us
  Pallas kernels: 122 us -> 109 us
    pallas_call x1, Pallas kernels: 122 us -> 109 us  [block(): pl.pallas_call(kernel, out_shape=jax.ShapeDtypeStruct((FRAMES, PATCHES, D...]
where the time goes in v4:
time: 112 us
  Pallas kernels  109 us (97%)
  local copies, waits for them, and re-layouts  2.37 us (2%)
    pallas_call x1, Pallas kernels, block(): pl.pallas_call(kernel, out_shape=jax.ShapeDtypeStruct((FRAMES, PATCHES, D...  109 us
    unnamed x1, local copies, waits for them, and re-layouts  2.37 us

profile of v4, /device:TPU:1, one launch (start us, length us, event | category | flops | bytes accessed | tf_op | source)
XLA Modules:
  0.0 111.8 jit_solution(16439982366044206419)
XLA Ops:
  0.0 109.4 %space_time_block.1 = bf16[4,128,1152]{2,1,0:T(8,128)(2,1)} custom-call(bf16[4,128,1152]{2,1,0:T(8,128)(2,1)} %video.1, s32[128]{0:T(128)} %row_index.1, s32[128]{0:T(128)} %col_index.1, s32[4]{0:T(128)} %frame_index.1, f32[1152]{0:T(1024)} %shift_s.1, f32[1152]{0:T(1024)} %scale_s.1, f32[1152]{0:T(1024)} %gate_s.1, bf16[1728,1152]{1,0:T(8,128)(2,1)} %bitcast.2, ...), custom_call_target="tpu_custom_call" | custom-call | tf_op jit(solution)/shard_map/space_time_block/pallas_call | solution.py:456
  109.4 2.4 %copy.18 = bf16[4,128,1152]{2,1,0:T(8,128)(2,1)} copy(bf16[4,128,1152]{2,1,0:T(8,128)(2,1)} %space_time_block.1) | data formatting | bytes 2359296

commit v5 on v4

--- a/solution.py
+++ b/solution.py
@@ -25,6 +25,7 @@
 LANES = 3 * INNER + HALF
 FACTOR = math.log2(math.e) / math.sqrt(HD)
 CHUNK = 512
+EARLY = 2
 EPSILON = 1e-06
 MESH = pl.DeviceIdType.MESH
 BF16 = jnp.bfloat16
@@ -59,7 +60,7 @@
     out,
     video_held, w_s_held, out_s_held, w_t_held, out_t_held,
     pos, z_recv, pos_recv, frame_recv, frame_rows, time_rows, time_tables,
-    x_send, x_recv, key_a, key_b, value_t, score_a, score_b, o_send, o_recv,
+    x_send, x_recv, key_a, key_b, value_t, score_a, score_b, early_top, early_sum, o_send, o_recv,
     t_send, t_recv, joined, total, r_send, r_recv,
     l_sem, z_ssem, z_rsem, p_ssem, p_rsem, f_ssem, f_rsem, x_ssem, x_rsem,
     o_ssem, o_rsem, t_ssem, t_rsem, r_ssem, r_rsem,
@@ -135,20 +136,34 @@
     for k in range(1, TM):
         frame_copy(k).start()
 
-    def x_copy(c, k):
+    def parts(c):
+        return [(c, slice(0, 3 * PAIR))] if c < 3 else [(3, slice(PAIR, 3 * PAIR)), (4, slice(0, PAIR))]
+
+    def x_copies(c, k):
         d = lax.rem(x + k, 4)
-        return remote(
-            x_send.at[c, d], x_recv.at[c, x], x_ssem.at[c, k], x_rsem.at[c, x], space=zh * 4 + d
-        )
+        return [
+            remote(
+                x_send.at[c, d, rows], x_recv.at[c, x, rows], x_ssem.at[n, k], x_rsem.at[n, x],
+                space=zh * 4 + d,
+            )
+            for n, rows in parts(c)
+        ]
+
+    def x_arrived(c, column, part):
+        n, rows = parts(c)[part]
+        remote(
+            x_send.at[c, column, rows], x_recv.at[c, column, rows], x_ssem.at[n, column],
+            x_rsem.at[n, column], space=zh * 4 + column,
+        ).wait_recv()
 
     head_row = lax.broadcasted_iota(jnp.int32, (PATCHES, PAIR), 1) < HD
 
     def place(c, column, held):
         rows = pl.ds(pl.multiple_of((c * 4 + column) * PATCHES, PATCHES), PATCHES)
-        keys = jnp.transpose(held[PAIR : 2 * PAIR].astype(F32))
+        keys = jnp.transpose(held[0:PAIR].astype(F32))
         key_a[rows] = jnp.where(head_row, keys, 0.0).astype(BF16)
         key_b[rows] = jnp.where(head_row, 0.0, keys).astype(BF16)
-        value_t[0:PAIR, rows] = held[2 * PAIR :]
+        value_t[0:PAIR, rows] = held[PAIR:]
 
     def project(first, streams, places):
         y = matmul_t(
@@ -178,21 +193,19 @@
                 rows = slice(2 * INNER + d * PAIR, 2 * INNER + (d + 1) * PAIR)
                 x_send[first + e, d, 2 * PAIR :] = part[rows].astype(BF16)
         for e in range(len(streams)):
-            for k in (1, 3, 2):
-                x_copy(first + e, k).start()
+            for part in range(len(parts(first + e))):
+                for k in (1, 3, 2):
+                    x_copies(first + e, k)[part].start()
         for e in range(len(streams)):
             c = first + e
-            place(c, x, x_send[c, x])
+            place(c, x, x_send[c, x, PAIR:])
             x_recv[c, x, 0:PAIR] = x_send[c, x, 0:PAIR]
 
     def gather(c):
         for k in (1, 3, 2):
             column = lax.rem(x + k, 4)
-            remote(
-                x_send.at[c, k], x_recv.at[c, column], x_ssem.at[c, k], x_rsem.at[c, column],
-                space=zh * 4 + column,
-            ).wait_recv()
-            place(c, column, x_recv[c, column])
+            x_arrived(c, column, 0)
+            place(c, column, x_recv[c, column, PAIR:])
 
     def z_arrived(slot):
         f = lax.rem(zh + (1, 3, 2)[slot], 4)
@@ -246,52 +259,95 @@
     z_arrived(0)
     z_arrived(1)
     project(1, [z_recv[0], z_recv[1]], [pos_recv[0], pos_recv[1]])
-    gather(1)
-    gather(2)
-    z_arrived(2)
-    project(3, [z_recv[2]], [pos_recv[2]])
-    gather(3)
-
     def o_copy(j):
         return remote(o_send.at[j], o_recv.at[space], o_ssem.at[j], o_rsem.at[space], space=j)
 
     pair_row = lax.broadcasted_iota(jnp.int32, (PAIR, 2 * PATCHES), 0) < HD
-    chunks = [slice(n * CHUNK, (n + 1) * CHUNK) for n in range(KEYS // CHUNK)]
-
-    def attend(n, carry):
-        c = 3 - n // 2
-        off = jnp.where(c == 3, 2, jnp.where(c == 2, 3, c))
-        first = lax.rem(n + x // 2 + 1, 2) * 2
-        queries = jnp.concatenate([x_recv[c, first, 0:PAIR], x_recv[c, first + 1, 0:PAIR]], axis=1)
+    heads = ((key_a, score_a), (key_b, score_b))
+
+    def queries_of(c, half):
+        return jnp.concatenate(
+            [x_recv[c, 2 * half, 0:PAIR], x_recv[c, 2 * half + 1, 0:PAIR]], axis=1
+        )
+
+    def score(queries, blocks):
         tops = []
-        for keys, scores in ((key_a, score_a), (key_b, score_b)):
+        for keys, scores in heads:
             top = None
-            for rows in chunks:
+            for n in blocks:
+                rows = slice(n * CHUNK, (n + 1) * CHUNK)
                 product = matmul(keys[rows], queries)
                 scores[rows] = product
                 high = jnp.max(product.reshape(CHUNK // 8, 8, 2 * PATCHES), axis=0)
                 top = high if top is None else jnp.maximum(top, high)
             tops.append(jnp.max(top, axis=0, keepdims=True))
-        mixed = []
-        for scores, top in zip((score_a, score_b), tops):
+        return tops
+
+    def mix(tops, blocks):
+        sums = []
+        for (_, scores), top in zip(heads, tops):
             both = None
-            for rows in chunks:
+            for n in blocks:
+                rows = slice(n * CHUNK, (n + 1) * CHUNK)
                 weights = jnp.exp2((scores[rows] - top) * FACTOR).astype(BF16)
                 product = matmul(value_t[:, rows], weights)
                 both = product if both is None else both + product
-            mixed.append(both[0:PAIR] / both[PAIR : PAIR + 1])
+            sums.append(both)
+        return sums
+
+    def early(n, carry):
+        tops = score(queries_of(n // 2, lax.rem(n, 2)), (0, 1, 2))
+        for h, (top, both) in enumerate(zip(tops, mix(tops, (0, 1, 2)))):
+            early_top[n, h] = jnp.broadcast_to(top, (8, 2 * PATCHES))
+            early_sum[n, h] = both
+        return carry
+
+    def finish(c, n):
+        half = lax.rem(n + x // 2 + 1, 2)
+        queries = queries_of(c, half)
+        if c == 3:
+            sums = mix(score(queries, (0, 1, 2, 3)), (0, 1, 2, 3))
+        else:
+            tops = []
+            scales = []
+            for h, top in enumerate(score(queries, (3,))):
+                old = early_top[2 * c + half, h, 0:1]
+                tops.append(jnp.maximum(old, top))
+                scales.append(jnp.exp2((old - tops[h]) * FACTOR))
+            sums = [
+                both + early_sum[2 * c + half, h] * scales[h]
+                for h, both in enumerate(mix(tops, (3,)))
+            ]
+        mixed = [both[0:PAIR] / both[PAIR : PAIR + 1] for both in sums]
         result = jnp.where(pair_row, mixed[0], mixed[1]).astype(BF16)
         for e in range(2):
-            j = lax.rem(zh + off, 4) * 4 + first + e
+            j = lax.rem(zh + (0, 1, 3, 2)[c], 4) * 4 + 2 * half + e
             o_send[j] = result[:, e * PATCHES : (e + 1) * PATCHES]
-
-            @pl.when(j != space)
-            def _():
+            if c:
                 o_copy(j).start()
-
-        return carry
-
-    lax.fori_loop(0, SPACE // 2, attend, 0)
+            else:
+
+                @pl.when(j != space)
+                def _():
+                    o_copy(j).start()
+
+    gather(1)
+    gather(2)
+    lax.fori_loop(0, EARLY, early, 0)
+    z_arrived(2)
+    project(3, [z_recv[2]], [pos_recv[2]])
+    lax.fori_loop(EARLY, 6, early, 0)
+    gather(3)
+    for c in (2, 1, 3, 0):
+        if c == 3:
+            for k in (1, 3, 2):
+                x_arrived(3, lax.rem(x + k, 4), 1)
+
+        def step(n, carry, c=c):
+            finish(c, n)
+            return carry
+
+        lax.fori_loop(0, 2, step, 0)
     o_recv[space] = o_send[space]
 
     def t_copy(i, d):
@@ -384,25 +440,29 @@
                 r_copy(s, r).start()
     r_recv[:, tm] = r_send[0, :, yc]
 
-    def r_arrived(k, carry):
-        j = lax.rem(tm + k, TM)
-        remote(r_send.at[0, :, 0], r_recv.at[:, j], r_ssem.at[j], r_rsem.at[j], tm=j).wait_recv()
-        return carry
-
-    lax.fori_loop(1, TM, r_arrived, 0)
     load_out_t.wait()
-    for i in range(2):
-        branch = matmul(r_recv[i].reshape(2 * PATCHES, WIDE), out_t_held[...])
-        stream = t_send[i].reshape(2 * PATCHES, D).astype(F32)
-        stream = (stream + gate_t[...].reshape(1, D) * branch).reshape(TM, 2, 8, D)
-        for e in range(2):
-            out[2 * i + e] = stream[:, e].reshape(PATCHES, D).astype(BF16)
+    for s in range(2):
+        for r in range(NEAR):
+            if (s, r) != (0, 0):
+                j = peer(s, r)
+                remote(
+                    r_send.at[0, :, 0], r_recv.at[:, j], r_ssem.at[j], r_rsem.at[j], tm=j
+                ).wait_recv()
+        near = pl.ds(side(s), NEAR)
+        branch = matmul(r_recv[:, near].reshape(2 * PATCHES, WIDE), out_t_held[...])
+        stream = t_send[:, near].reshape(2 * PATCHES, D).astype(F32)
+        stream = (stream + gate_t[...].reshape(1, D) * branch).reshape(2, NEAR, 2, 8, D)
+        patches = pl.ds(pl.multiple_of(side(s) * 8, 64), 64)
+        for i in range(2):
+            for e in range(2):
+                out[2 * i + e, patches] = stream[i, :, e].reshape(64, D).astype(BF16)
 
     z_copy(2)[0].wait_send()
     for n in range(3):
         z_copy(n)[1].wait_send()
         for c in range(4):
-            x_copy(c, n + 1).wait_send()
+            for copy in x_copies(c, n + 1):
+                copy.wait_send()
 
     def o_sent(k, carry):
         o_copy(lax.rem(space + k, SPACE)).wait_send()
@@ -442,6 +502,8 @@
         ((PAIR + 16, KEYS), BF16),
         ((KEYS, 2 * PATCHES), F32),
         ((KEYS, 2 * PATCHES), F32),
+        ((6, 2, 8, 2 * PATCHES), F32),
+        ((6, 2, PAIR + 16, 2 * PATCHES), F32),
         ((SPACE, PAIR, PATCHES), BF16),
         ((SPACE, PAIR, PATCHES), BF16),
         ((2, TM, 16, D), BF16),
@@ -451,7 +513,7 @@
         ((2, 2, NEAR, 16, WIDE), BF16),
         ((2, TM, 16, WIDE), BF16),
     ]
-    sems = [(10,), (3,), (3,), (3,), (3,), (TM,), (TM,), (4, 4), (4, 4)]
+    sems = [(10,), (3,), (3,), (3,), (3,), (TM,), (TM,), (5, 4), (5, 4)]
     sems += [(SPACE,), (SPACE,), (2, TM), (2, TM), (TM,), (TM,)]
     return pl.pallas_call(
         kernel,

time: 112 us -> 106 us (0.946)
  Pallas kernels: 109 us -> 103 us
    pallas_call x1, Pallas kernels: 109 us -> 103 us  [block(): pl.pallas_call(kernel, out_shape=jax.ShapeDtypeStruct((FRAMES, PATCHES, D...]
where the time goes in v5:
time: 106 us; the launch traced here: 105 us
  Pallas kernels  103 us (97%)
  local copies, waits for them, and re-layouts  2.37 us (2%)
    pallas_call x1, Pallas kernels, block(): pl.pallas_call(kernel, out_shape=jax.ShapeDtypeStruct((FRAMES, PATCHES, D...  103 us
    unnamed x1, local copies, waits for them, and re-layouts  2.37 us

profile of v5, /device:TPU:1, one launch (start us, length us, event | category | flops | bytes accessed | tf_op | source)
XLA Modules:
  0.0 105.4 jit_solution(15944427626505153226)
XLA Ops:
  0.0 103.0 %space_time_block.1 = bf16[4,128,1152]{2,1,0:T(8,128)(2,1)} custom-call(bf16[4,128,1152]{2,1,0:T(8,128)(2,1)} %video.1, s32[128]{0:T(128)} %row_index.1, s32[128]{0:T(128)} %col_index.1, s32[4]{0:T(128)} %frame_index.1, f32[1152]{0:T(1024)} %shift_s.1, f32[1152]{0:T(1024)} %scale_s.1, f32[1152]{0:T(1024)} %gate_s.1, bf16[1728,1152]{1,0:T(8,128)(2,1)} %bitcast.2, ...), custom_call_target="tpu_custom_call" | custom-call | tf_op jit(solution)/shard_map/space_time_block/pallas_call | solution.py:518
  103.0 2.4 %copy.18 = bf16[4,128,1152]{2,1,0:T(8,128)(2,1)} copy(bf16[4,128,1152]{2,1,0:T(8,128)(2,1)} %space_time_block.1) | data formatting | bytes 2359296

commit v6 on v5

--- a/solution.py
+++ b/solution.py
@@ -25,7 +25,6 @@
 LANES = 3 * INNER + HALF
 FACTOR = math.log2(math.e) / math.sqrt(HD)
 CHUNK = 512
-EARLY = 2
 EPSILON = 1e-06
 MESH = pl.DeviceIdType.MESH
 BF16 = jnp.bfloat16
@@ -55,13 +54,15 @@
 
 
 def kernel(
-    video, row_index, col_index, frame_index,
-    shift_s, scale_s, gate_s, w_s, out_s, shift_t, scale_t, gate_t, w_t, out_t, table_s, table_t,
+    video, row_index_in, col_index_in, frame_index,
+    shift_s_in, scale_s_in, gate_s_in, w_s, out_s, shift_t_in, scale_t_in, gate_t_in, w_t, out_t,
+    table_s_in, table_t_in,
     out,
+    row_index, col_index, shift_s, scale_s, gate_s, shift_t, scale_t, gate_t, table_s, table_t,
     video_held, w_s_held, out_s_held, w_t_held, out_t_held,
     pos, z_recv, pos_recv, frame_recv, frame_rows, time_rows, time_tables,
     x_send, x_recv, key_a, key_b, value_t, score_a, score_b, early_top, early_sum, o_send, o_recv,
-    t_send, t_recv, joined, total, r_send, r_recv,
+    t_send, t_recv, joined, total, r_send, r_recv, result,
     l_sem, z_ssem, z_rsem, p_ssem, p_rsem, f_ssem, f_rsem, x_ssem, x_rsem,
     o_ssem, o_rsem, t_ssem, t_rsem, r_ssem, r_rsem,
 ):
@@ -90,6 +91,16 @@
         copy.start()
         return copy
 
+    small = [
+        load(10 + n, *pair)
+        for n, pair in enumerate(
+            (
+                (row_index_in, row_index), (col_index_in, col_index), (table_s_in, table_s),
+                (shift_s_in, shift_s), (scale_s_in, scale_s), (table_t_in, table_t),
+                (gate_s_in, gate_s), (shift_t_in, shift_t), (scale_t_in, scale_t), (gate_t_in, gate_t),
+            )
+        )
+    ]
     load_own = load(0, video.at[zh], video_held.at[zh])
     load_w_s = load(1, w_s, w_s_held)
     load_rest = [
@@ -103,6 +114,27 @@
     ]
     load_out_t = load(9, out_t, out_t_held.at[pl.ds(HALF, INNER)])
 
+    def z_copy(n):
+        f = lax.rem(zh + (1, 3, 2)[n], 4)
+        to = {"space": f * 4 + x}
+        slot = (1, 0, 2)[n]
+        return (
+            remote(video.at[f], z_recv.at[slot], z_ssem.at[n], z_rsem.at[slot], **to),
+            remote(pos, pos_recv.at[slot], p_ssem.at[n], p_rsem.at[slot], **to),
+        )
+
+    def frame_copy(k):
+        d = lax.rem(tm + k, TM)
+        return remote(
+            frame_recv.at[tm], frame_recv.at[tm], f_ssem.at[d], f_rsem.at[tm], tm=d
+        )
+
+    pl.semaphore_wait(barrier, SPACE + TM - 2)
+    for n in range(2):
+        z_copy(n)[0].start()
+    for copy in small:
+        copy.wait()
+
     row = lax.broadcasted_iota(jnp.int32, (8, PATCHES), 0)
     here = jnp.where(
         row == 0, row_index[...].reshape(1, PATCHES), col_index[...].reshape(1, PATCHES)
@@ -113,24 +145,6 @@
         times = jnp.where(row == f, frame_index[f], times)
     frame_recv[tm] = times.astype(F32)
 
-    def z_copy(n):
-        f = lax.rem(zh + (1, 3, 2)[n], 4)
-        to = {"space": f * 4 + x}
-        slot = (1, 0, 2)[n]
-        return (
-            remote(video.at[f], z_recv.at[slot], z_ssem.at[n], z_rsem.at[slot], **to),
-            remote(pos, pos_recv.at[slot], p_ssem.at[n], p_rsem.at[slot], **to),
-        )
-
-    def frame_copy(k):
-        d = lax.rem(tm + k, TM)
-        return remote(
-            frame_recv.at[tm], frame_recv.at[tm], f_ssem.at[d], f_rsem.at[tm], tm=d
-        )
-
-    pl.semaphore_wait(barrier, SPACE + TM - 2)
-    for n in range(2):
-        z_copy(n)[0].start()
     for n in range(3):
         z_copy(n)[1].start()
     for k in range(1, TM):
@@ -296,7 +310,7 @@
         return sums
 
     def early(n, carry):
-        tops = score(queries_of(n // 2, lax.rem(n, 2)), (0, 1, 2))
+        tops = score(queries_of(n // 2 + 1, lax.rem(n, 2)), (0, 1, 2))
         for h, (top, both) in enumerate(zip(tops, mix(tops, (0, 1, 2)))):
             early_top[n, h] = jnp.broadcast_to(top, (8, 2 * PATCHES))
             early_sum[n, h] = both
@@ -305,17 +319,17 @@
     def finish(c, n):
         half = lax.rem(n + x // 2 + 1, 2)
         queries = queries_of(c, half)
-        if c == 3:
+        if c in (0, 3):
             sums = mix(score(queries, (0, 1, 2, 3)), (0, 1, 2, 3))
         else:
             tops = []
             scales = []
             for h, top in enumerate(score(queries, (3,))):
-                old = early_top[2 * c + half, h, 0:1]
+                old = early_top[2 * c - 2 + half, h, 0:1]
                 tops.append(jnp.maximum(old, top))
                 scales.append(jnp.exp2((old - tops[h]) * FACTOR))
             sums = [
-                both + early_sum[2 * c + half, h] * scales[h]
+                both + early_sum[2 * c - 2 + half, h] * scales[h]
                 for h, both in enumerate(mix(tops, (3,)))
             ]
         mixed = [both[0:PAIR] / both[PAIR : PAIR + 1] for both in sums]
@@ -331,12 +345,11 @@
                 def _():
                     o_copy(j).start()
 
+    z_arrived(2)
+    project(3, [z_recv[2]], [pos_recv[2]])
     gather(1)
     gather(2)
-    lax.fori_loop(0, EARLY, early, 0)
-    z_arrived(2)
-    project(3, [z_recv[2]], [pos_recv[2]])
-    lax.fori_loop(EARLY, 6, early, 0)
+    lax.fori_loop(0, 4, early, 0)
     gather(3)
     for c in (2, 1, 3, 0):
         if c == 3:
@@ -441,6 +454,7 @@
     r_recv[:, tm] = r_send[0, :, yc]
 
     load_out_t.wait()
+    stores = []
     for s in range(2):
         for r in range(NEAR):
             if (s, r) != (0, 0):
@@ -455,8 +469,13 @@
         patches = pl.ds(pl.multiple_of(side(s) * 8, 64), 64)
         for i in range(2):
             for e in range(2):
-                out[2 * i + e, patches] = stream[i, :, e].reshape(64, D).astype(BF16)
-
+                result[2 * i + e, patches] = stream[i, :, e].reshape(64, D).astype(BF16)
+        store = pltpu.make_async_copy(result.at[:, patches], out.at[:, patches], l_sem.at[s])
+        store.start()
+        stores.append(store)
+
+    for store in stores:
+        store.wait()
     z_copy(2)[0].wait_send()
     for n in range(3):
         z_copy(n)[1].wait_send()
@@ -477,12 +496,12 @@
 
 
 def block(*arrays):
-    vmem = pl.BlockSpec(memory_space=pltpu.VMEM)
     smem = pl.BlockSpec(memory_space=pltpu.SMEM)
     hbm = pl.BlockSpec(memory_space=pl.ANY)
     dma = pltpu.SemaphoreType.DMA
-    specs = [hbm, vmem, vmem, smem] + [vmem, vmem, vmem, hbm, hbm] * 2 + [vmem, vmem]
-    held = [
+    specs = [hbm, hbm, hbm, smem] + [hbm] * 12
+    held = [((PATCHES,), jnp.int32)] * 2 + [((D,), F32)] * 6 + [((HD, 8), F32), ((8, WIDE), F32)]
+    held += [
         ((FRAMES, PATCHES, D), BF16),
         ((3 * INNER, D), BF16),
         ((INNER, D), BF16),
@@ -502,8 +521,8 @@
         ((PAIR + 16, KEYS), BF16),
         ((KEYS, 2 * PATCHES), F32),
         ((KEYS, 2 * PATCHES), F32),
-        ((6, 2, 8, 2 * PATCHES), F32),
-        ((6, 2, PAIR + 16, 2 * PATCHES), F32),
+        ((4, 2, 8, 2 * PATCHES), F32),
+        ((4, 2, PAIR + 16, 2 * PATCHES), F32),
         ((SPACE, PAIR, PATCHES), BF16),
         ((SPACE, PAIR, PATCHES), BF16),
         ((2, TM, 16, D), BF16),
@@ -512,14 +531,15 @@
         ((256, WIDE), F32),
         ((2, 2, NEAR, 16, WIDE), BF16),
         ((2, TM, 16, WIDE), BF16),
+        ((FRAMES, PATCHES, D), BF16),
     ]
-    sems = [(10,), (3,), (3,), (3,), (3,), (TM,), (TM,), (5, 4), (5, 4)]
+    sems = [(20,), (3,), (3,), (3,), (3,), (TM,), (TM,), (5, 4), (5, 4)]
     sems += [(SPACE,), (SPACE,), (2, TM), (2, TM), (TM,), (TM,)]
     return pl.pallas_call(
         kernel,
         out_shape=jax.ShapeDtypeStruct((FRAMES, PATCHES, D), BF16),
         in_specs=specs,
-        out_specs=vmem,
+        out_specs=hbm,
         scratch_shapes=[pltpu.VMEM(*h) for h in held] + [dma(s) for s in sems],
         compiler_params=pltpu.CompilerParams(
             collective_id=1, has_side_effects=True, vmem_limit_bytes=56 * 2**20

time: 106 us -> 104 us (0.981)
  Pallas kernels: 103 us -> 101 us
    pallas_call x1, Pallas kernels: 103 us -> 101 us  [block(): pl.pallas_call(kernel, out_shape=jax.ShapeDtypeStruct((FRAMES, PATCHES, D...]
where the time goes in v6:
time: 104 us
  Pallas kernels  101 us (97%)
  local copies, waits for them, and re-layouts  2.37 us (2%)
    pallas_call x1, Pallas kernels, block(): pl.pallas_call(kernel, out_shape=jax.ShapeDtypeStruct((FRAMES, PATCHES, D...  101 us
    unnamed x1, local copies, waits for them, and re-layouts  2.37 us

profile of v6, /device:TPU:1, one launch (start us, length us, event | category | flops | bytes accessed | tf_op | source)
XLA Modules:
  0.0 103.8 jit_solution(13974827367713806082)
XLA Ops:
  0.0 101.5 %space_time_block.1 = bf16[4,128,1152]{2,1,0:T(8,128)(2,1)} custom-call(bf16[4,128,1152]{2,1,0:T(8,128)(2,1)} %video.1, s32[128]{0:T(128)} %row_index_in.1, s32[128]{0:T(128)} %col_index_in.1, s32[4]{0:T(128)} %frame_index.1, f32[1152]{0:T(1024)} %shift_s_in.1, f32[1152]{0:T(1024)} %scale_s_in.1, f32[1152]{0:T(1024)} %gate_s_in.1, ...), custom_call_target="tpu_custom_call" | custom-call | tf_op jit(solution)/shard_map/space_time_block/pallas_call | solution.py:538
  101.5 2.4 %copy.18 = bf16[4,128,1152]{2,1,0:T(8,128)(2,1)} copy(bf16[4,128,1152]{2,1,0:T(8,128)(2,1)} %space_time_block.1) | data formatting | bytes 2359296

commit v7 on v6

--- a/solution.py
+++ b/solution.py
@@ -61,7 +61,7 @@
     row_index, col_index, shift_s, scale_s, gate_s, shift_t, scale_t, gate_t, table_s, table_t,
     video_held, w_s_held, out_s_held, w_t_held, out_t_held,
     pos, z_recv, pos_recv, frame_recv, frame_rows, time_rows, time_tables,
-    x_send, x_recv, key_a, key_b, value_t, score_a, score_b, early_top, early_sum, o_send, o_recv,
+    x_send, x_recv, key_a, key_b, value_t, score_a, score_b, o_send, o_recv,
     t_send, t_recv, joined, total, r_send, r_recv, result,
     l_sem, z_ssem, z_rsem, p_ssem, p_rsem, f_ssem, f_rsem, x_ssem, x_rsem,
     o_ssem, o_rsem, t_ssem, t_rsem, r_ssem, r_rsem,
@@ -101,11 +101,14 @@
             )
         )
     ]
-    load_own = load(0, video.at[zh], video_held.at[zh])
+    load_own, load_far = (
+        load(2 * k, video.at[lax.rem(zh + 2 * k, 4)], video_held.at[lax.rem(zh + 2 * k, 4)])
+        for k in range(2)
+    )
     load_w_s = load(1, w_s, w_s_held)
     load_rest = [
-        load(1 + k, video.at[lax.rem(zh + k, 4)], video_held.at[lax.rem(zh + k, 4)])
-        for k in range(1, 4)
+        load(3 + k, video.at[lax.rem(zh + 1 + 2 * k, 4)], video_held.at[lax.rem(zh + 1 + 2 * k, 4)])
+        for k in range(2)
     ]
     load_out_s = load(5, out_s, out_s_held)
     load_w_t = [
@@ -115,9 +118,9 @@
     load_out_t = load(9, out_t, out_t_held.at[pl.ds(HALF, INNER)])
 
     def z_copy(n):
-        f = lax.rem(zh + (1, 3, 2)[n], 4)
+        f = lax.rem(zh + (1, 3)[n], 4)
         to = {"space": f * 4 + x}
-        slot = (1, 0, 2)[n]
+        slot = 1 - n
         return (
             remote(video.at[f], z_recv.at[slot], z_ssem.at[n], z_rsem.at[slot], **to),
             remote(pos, pos_recv.at[slot], p_ssem.at[n], p_rsem.at[slot], **to),
@@ -145,29 +148,29 @@
         times = jnp.where(row == f, frame_index[f], times)
     frame_recv[tm] = times.astype(F32)
 
-    for n in range(3):
+    for n in range(2):
         z_copy(n)[1].start()
-    for k in range(1, TM):
-        frame_copy(k).start()
 
     def parts(c):
         return [(c, slice(0, 3 * PAIR))] if c < 3 else [(3, slice(PAIR, 3 * PAIR)), (4, slice(0, PAIR))]
 
     def x_copies(c, k):
         d = lax.rem(x + k, 4)
+        to = lax.rem(zh + 2, 4) if c == 3 else zh
         return [
             remote(
                 x_send.at[c, d, rows], x_recv.at[c, x, rows], x_ssem.at[n, k], x_rsem.at[n, x],
-                space=zh * 4 + d,
+                space=to * 4 + d,
             )
             for n, rows in parts(c)
         ]
 
     def x_arrived(c, column, part):
         n, rows = parts(c)[part]
+        to = lax.rem(zh + 2, 4) if c == 3 else zh
         remote(
             x_send.at[c, column, rows], x_recv.at[c, column, rows], x_ssem.at[n, column],
-            x_rsem.at[n, column], space=zh * 4 + column,
+            x_rsem.at[n, column], space=to * 4 + column,
         ).wait_recv()
 
     head_row = lax.broadcasted_iota(jnp.int32, (PATCHES, PAIR), 1) < HD
@@ -179,7 +182,7 @@
         key_b[rows] = jnp.where(head_row, 0.0, keys).astype(BF16)
         value_t[0:PAIR, rows] = held[PAIR:]
 
-    def project(first, streams, places):
+    def project(blocks, streams, places):
         y = matmul_t(
             w_s_held[...],
             jnp.concatenate(
@@ -201,41 +204,54 @@
             for d in range(4):
                 for n in range(2):
                     base = n * HEADS + 2 * d
-                    x_send[first + e, d, n * PAIR : (n + 1) * PAIR] = jnp.concatenate(
+                    x_send[blocks[e], d, n * PAIR : (n + 1) * PAIR] = jnp.concatenate(
                         [turned(base), turned(base + 1)], axis=0
                     ).astype(BF16)
                 rows = slice(2 * INNER + d * PAIR, 2 * INNER + (d + 1) * PAIR)
-                x_send[first + e, d, 2 * PAIR :] = part[rows].astype(BF16)
-        for e in range(len(streams)):
-            for part in range(len(parts(first + e))):
+                x_send[blocks[e], d, 2 * PAIR :] = part[rows].astype(BF16)
+        for c in blocks:
+            if c < 3:
                 for k in (1, 3, 2):
-                    x_copies(first + e, k)[part].start()
-        for e in range(len(streams)):
-            c = first + e
-            place(c, x, x_send[c, x, PAIR:])
-            x_recv[c, x, 0:PAIR] = x_send[c, x, 0:PAIR]
+                    x_copies(c, k)[0].start()
+        for c in blocks:
+            if c < 3:
+                place(c, x, x_send[c, x, PAIR:])
+                x_recv[c, x, 0:PAIR] = x_send[c, x, 0:PAIR]
 
     def gather(c):
-        for k in (1, 3, 2):
+        for k in (0, 1, 3, 2) if c == 3 else (1, 3, 2):
             column = lax.rem(x + k, 4)
             x_arrived(c, column, 0)
             place(c, column, x_recv[c, column, PAIR:])
 
     def z_arrived(slot):
-        f = lax.rem(zh + (1, 3, 2)[slot], 4)
+        f = lax.rem(zh + (1, 3)[slot], 4)
         to = {"space": f * 4 + x}
         remote(video.at[f], z_recv.at[slot], z_ssem.at[slot], z_rsem.at[slot], **to).wait_recv()
         remote(pos, pos_recv.at[slot], p_ssem.at[slot], p_rsem.at[slot], **to).wait_recv()
 
     load_own.wait()
+    load_far.wait()
     load_w_s.wait()
-    project(0, [video_held[zh]], [pos[...]])
+    project((0, 3), [video_held[zh], video_held[lax.rem(zh + 2, 4)]], [pos[...], pos[...]])
 
     w_t_held[3 * INNER :] = jnp.zeros((HALF, D), BF16)
     out_t_held[0:HALF] = jnp.zeros((HALF, D), BF16)
     value_t[PAIR:] = jnp.where(
         lax.broadcasted_iota(jnp.int32, (16, KEYS), 0) == 0, 1.0, 0.0
     ).astype(BF16)
+
+    for n in range(2):
+        z_copy(n)[0].wait_send()
+    for part in range(2):
+        for k in range(4):
+            x_copies(3, k)[part].start()
+    for k in range(1, TM):
+        frame_copy(k).start()
+    gather(0)
+    z_arrived(0)
+    z_arrived(1)
+    project((1, 2), [z_recv[0], z_recv[1]], [pos_recv[0], pos_recv[1]])
 
     def frame_arrived(k, carry):
         j = lax.rem(tm + k, TM)
@@ -266,101 +282,53 @@
 
     lax.fori_loop(0, 64, widen, 0)
 
-    for n in range(2):
-        z_copy(n)[0].wait_send()
-    z_copy(2)[0].start()
-    gather(0)
-    z_arrived(0)
-    z_arrived(1)
-    project(1, [z_recv[0], z_recv[1]], [pos_recv[0], pos_recv[1]])
+    gather(1)
+    gather(2)
+    gather(3)
+
     def o_copy(j):
         return remote(o_send.at[j], o_recv.at[space], o_ssem.at[j], o_rsem.at[space], space=j)
 
     pair_row = lax.broadcasted_iota(jnp.int32, (PAIR, 2 * PATCHES), 0) < HD
-    heads = ((key_a, score_a), (key_b, score_b))
-
-    def queries_of(c, half):
-        return jnp.concatenate(
-            [x_recv[c, 2 * half, 0:PAIR], x_recv[c, 2 * half + 1, 0:PAIR]], axis=1
-        )
-
-    def score(queries, blocks):
+    chunks = [slice(n * CHUNK, (n + 1) * CHUNK) for n in range(KEYS // CHUNK)]
+
+    def attend(n, carry):
+        c = jnp.where(n < 4, 2 - n // 2, jnp.where(n < 6, 3, 0))
+        off = jnp.where(c == 3, 2, jnp.where(c == 2, 3, c))
+        first = lax.rem(n + x // 2 + 1, 2) * 2
+        queries = jnp.concatenate([x_recv[c, first, 0:PAIR], x_recv[c, first + 1, 0:PAIR]], axis=1)
         tops = []
-        for keys, scores in heads:
+        for keys, scores in ((key_a, score_a), (key_b, score_b)):
             top = None
-            for n in blocks:
-                rows = slice(n * CHUNK, (n + 1) * CHUNK)
+            for rows in chunks:
                 product = matmul(keys[rows], queries)
                 scores[rows] = product
                 high = jnp.max(product.reshape(CHUNK // 8, 8, 2 * PATCHES), axis=0)
                 top = high if top is None else jnp.maximum(top, high)
             tops.append(jnp.max(top, axis=0, keepdims=True))
-        return tops
-
-    def mix(tops, blocks):
-        sums = []
-        for (_, scores), top in zip(heads, tops):
+        mixed = []
+        for scores, top in zip((score_a, score_b), tops):
             both = None
-            for n in blocks:
-                rows = slice(n * CHUNK, (n + 1) * CHUNK)
+            for rows in chunks:
                 weights = jnp.exp2((scores[rows] - top) * FACTOR).astype(BF16)
                 product = matmul(value_t[:, rows], weights)
                 both = product if both is None else both + product
-            sums.append(both)
-        return sums
-
-    def early(n, carry):
-        tops = score(queries_of(n // 2 + 1, lax.rem(n, 2)), (0, 1, 2))
-        for h, (top, both) in enumerate(zip(tops, mix(tops, (0, 1, 2)))):
-            early_top[n, h] = jnp.broadcast_to(top, (8, 2 * PATCHES))
-            early_sum[n, h] = both
-        return carry
-
-    def finish(c, n):
-        half = lax.rem(n + x // 2 + 1, 2)
-        queries = queries_of(c, half)
-        if c in (0, 3):
-            sums = mix(score(queries, (0, 1, 2, 3)), (0, 1, 2, 3))
-        else:
-            tops = []
-            scales = []
-            for h, top in enumerate(score(queries, (3,))):
-                old = early_top[2 * c - 2 + half, h, 0:1]
-                tops.append(jnp.maximum(old, top))
-                scales.append(jnp.exp2((old - tops[h]) * FACTOR))
-            sums = [
-                both + early_sum[2 * c - 2 + half, h] * scales[h]
-                for h, both in enumerate(mix(tops, (3,)))
-            ]
-        mixed = [both[0:PAIR] / both[PAIR : PAIR + 1] for both in sums]
+            mixed.append(both[0:PAIR] / both[PAIR : PAIR + 1])
         result = jnp.where(pair_row, mixed[0], mixed[1]).astype(BF16)
         for e in range(2):
-            j = lax.rem(zh + (0, 1, 3, 2)[c], 4) * 4 + 2 * half + e
+            j = lax.rem(zh + off, 4) * 4 + first + e
             o_send[j] = result[:, e * PATCHES : (e + 1) * PATCHES]
-            if c:
+
+            @pl.when(j != space)
+            def _():
                 o_copy(j).start()
-            else:
-
-                @pl.when(j != space)
-                def _():
-                    o_copy(j).start()
-
-    z_arrived(2)
-    project(3, [z_recv[2]], [pos_recv[2]])
-    gather(1)
-    gather(2)
-    lax.fori_loop(0, 4, early, 0)
-    gather(3)
-    for c in (2, 1, 3, 0):
-        if c == 3:
-            for k in (1, 3, 2):
-                x_arrived(3, lax.rem(x + k, 4), 1)
-
-        def step(n, carry, c=c):
-            finish(c, n)
-            return carry
-
-        lax.fori_loop(0, 2, step, 0)
+
+        return carry
+
+    lax.fori_loop(0, 4, attend, 0)
+    for k in range(4):
+        x_arrived(3, lax.rem(x + k, 4), 1)
+    lax.fori_loop(4, 8, attend, 0)
     o_recv[space] = o_send[space]
 
     def t_copy(i, d):
@@ -476,11 +444,11 @@
 
     for store in stores:
         store.wait()
-    z_copy(2)[0].wait_send()
-    for n in range(3):
+    for n in range(2):
         z_copy(n)[1].wait_send()
-        for c in range(4):
-            for copy in x_copies(c, n + 1):
+    for c in range(4):
+        for k in range(0 if c == 3 else 1, 4):
+            for copy in x_copies(c, k):
                 copy.wait_send()
 
     def o_sent(k, carry):
@@ -508,8 +476,8 @@
         ((LANES, D), BF16),
         ((WIDE, D), BF16),
         ((8, PATCHES), F32),
-        ((3, PATCHES, D), BF16),
-        ((3, 8, PATCHES), F32),
+        ((2, PATCHES, D), BF16),
+        ((2, 8, PATCHES), F32),
         ((TM, 8, 128), F32),
         ((64, 128), F32),
         ((3, 64, WIDE), F32),
@@ -521,8 +489,6 @@
         ((PAIR + 16, KEYS), BF16),
         ((KEYS, 2 * PATCHES), F32),
         ((KEYS, 2 * PATCHES), F32),
-        ((4, 2, 8, 2 * PATCHES), F32),
-        ((4, 2, PAIR + 16, 2 * PATCHES), F32),
         ((SPACE, PAIR, PATCHES), BF16),
         ((SPACE, PAIR, PATCHES), BF16),
         ((2, TM, 16, D), BF16),
@@ -533,7 +499,7 @@
         ((2, TM, 16, WIDE), BF16),
         ((FRAMES, PATCHES, D), BF16),
     ]
-    sems = [(20,), (3,), (3,), (3,), (3,), (TM,), (TM,), (5, 4), (5, 4)]
+    sems = [(20,), (2,), (2,), (2,), (2,), (TM,), (TM,), (5, 4), (5, 4)]
     sems += [(SPACE,), (SPACE,), (2, TM), (2, TM), (TM,), (TM,)]
     return pl.pallas_call(
         kernel,

time: 104 us -> 104 us (level)
  no operation moved by 1% of the time
where the time goes in v7:
time: 104 us; the launch traced here: 103 us
  Pallas kernels  101 us (97%)
  local copies, waits for them, and re-layouts  2.37 us (2%)
    pallas_call x1, Pallas kernels, block(): pl.pallas_call(kernel, out_shape=jax.ShapeDtypeStruct((FRAMES, PATCHES, D...  101 us
    unnamed x1, local copies, waits for them, and re-layouts  2.37 us

profile of v7, /device:TPU:1, one launch (start us, length us, event | category | flops | bytes accessed | tf_op | source)
XLA Modules:
  0.0 103.2 jit_solution(18145017583971300937)
XLA Ops:
  0.0 100.8 %space_time_block.1 = bf16[4,128,1152]{2,1,0:T(8,128)(2,1)} custom-call(bf16[4,128,1152]{2,1,0:T(8,128)(2,1)} %video.1, s32[128]{0:T(128)} %row_index_in.1, s32[128]{0:T(128)} %col_index_in.1, s32[4]{0:T(128)} %frame_index.1, f32[1152]{0:T(1024)} %shift_s_in.1, f32[1152]{0:T(1024)} %scale_s_in.1, f32[1152]{0:T(1024)} %gate_s_in.1, ...), custom_call_target="tpu_custom_call" | custom-call | tf_op jit(solution)/shard_map/space_time_block/pallas_call | solution.py:504
  100.8 2.4 %copy.18 = bf16[4,128,1152]{2,1,0:T(8,128)(2,1)} copy(bf16[4,128,1152]{2,1,0:T(8,128)(2,1)} %space_time_block.1) | data formatting | bytes 2359296

commit v8 on v7

--- a/solution.py
+++ b/solution.py
@@ -24,6 +24,7 @@
 WIDE = INNER + HALF
 LANES = 3 * INNER + HALF
 FACTOR = math.log2(math.e) / math.sqrt(HD)
+SIDE = PATCHES // 2
 CHUNK = 512
 EPSILON = 1e-06
 MESH = pl.DeviceIdType.MESH
@@ -61,7 +62,7 @@
     row_index, col_index, shift_s, scale_s, gate_s, shift_t, scale_t, gate_t, table_s, table_t,
     video_held, w_s_held, out_s_held, w_t_held, out_t_held,
     pos, z_recv, pos_recv, frame_recv, frame_rows, time_rows, time_tables,
-    x_send, x_recv, key_a, key_b, value_t, score_a, score_b, o_send, o_recv,
+    x_send, x_recv, key_a, key_b, value_t, score_a, score_b, early_top, early_sum, o_send, o_recv,
     t_send, t_recv, joined, total, r_send, r_recv, result,
     l_sem, z_ssem, z_rsem, p_ssem, p_rsem, f_ssem, f_rsem, x_ssem, x_rsem,
     o_ssem, o_rsem, t_ssem, t_rsem, r_ssem, r_rsem,
@@ -117,14 +118,17 @@
     ]
     load_out_t = load(9, out_t, out_t_held.at[pl.ds(HALF, INNER)])
 
-    def z_copy(n):
+    def near_copy(h, n):
         f = lax.rem(zh + (1, 3)[n], 4)
-        to = {"space": f * 4 + x}
-        slot = 1 - n
-        return (
-            remote(video.at[f], z_recv.at[slot], z_ssem.at[n], z_rsem.at[slot], **to),
-            remote(pos, pos_recv.at[slot], p_ssem.at[n], p_rsem.at[slot], **to),
-        )
+        return remote(
+            video.at[f, h * SIDE : (h + 1) * SIDE],
+            z_recv.at[h, (1 - n) * SIDE : (2 - n) * SIDE],
+            z_ssem.at[h, n], z_rsem.at[h, 1 - n], space=f * 4 + x,
+        )
+
+    def pos_copy(n):
+        f = lax.rem(zh + (1, 3)[n], 4)
+        return remote(pos, pos_recv.at[1 - n], p_ssem.at[n], p_rsem.at[1 - n], space=f * 4 + x)
 
     def frame_copy(k):
         d = lax.rem(tm + k, TM)
@@ -134,7 +138,7 @@
 
     pl.semaphore_wait(barrier, SPACE + TM - 2)
     for n in range(2):
-        z_copy(n)[0].start()
+        near_copy(0, n).start()
     for copy in small:
         copy.wait()
 
@@ -149,7 +153,7 @@
     frame_recv[tm] = times.astype(F32)
 
     for n in range(2):
-        z_copy(n)[1].start()
+        pos_copy(n).start()
 
     def parts(c):
         return [(c, slice(0, 3 * PAIR))] if c < 3 else [(3, slice(PAIR, 3 * PAIR)), (4, slice(0, PAIR))]
@@ -224,11 +228,22 @@
             x_arrived(c, column, 0)
             place(c, column, x_recv[c, column, PAIR:])
 
-    def z_arrived(slot):
-        f = lax.rem(zh + (1, 3)[slot], 4)
-        to = {"space": f * 4 + x}
-        remote(video.at[f], z_recv.at[slot], z_ssem.at[slot], z_rsem.at[slot], **to).wait_recv()
-        remote(pos, pos_recv.at[slot], p_ssem.at[slot], p_rsem.at[slot], **to).wait_recv()
+    def near_arrived(h):
+        for slot in range(2):
+            f = lax.rem(zh + (1, 3)[slot], 4)
+            remote(
+                video.at[f, 0:SIDE], z_recv.at[h, slot * SIDE : (slot + 1) * SIDE],
+                z_ssem.at[h, slot], z_rsem.at[h, slot], space=f * 4 + x,
+            ).wait_recv()
+            if h == 0:
+                remote(
+                    pos, pos_recv.at[slot], p_ssem.at[slot], p_rsem.at[slot], space=f * 4 + x
+                ).wait_recv()
+
+    def project_near(h):
+        lanes = slice(h * SIDE, (h + 1) * SIDE)
+        at = jnp.concatenate([pos_recv[0][:, lanes], pos_recv[1][:, lanes]], axis=1)
+        project((1 + h,), [z_recv[h]], [at])
 
     load_own.wait()
     load_far.wait()
@@ -242,16 +257,21 @@
     ).astype(BF16)
 
     for n in range(2):
-        z_copy(n)[0].wait_send()
+        near_copy(0, n).wait_send()
+    for n in range(2):
+        near_copy(1, n).start()
+    gather(0)
+    near_arrived(0)
+    project_near(0)
+    for n in range(2):
+        near_copy(1, n).wait_send()
     for part in range(2):
         for k in range(4):
             x_copies(3, k)[part].start()
     for k in range(1, TM):
         frame_copy(k).start()
-    gather(0)
-    z_arrived(0)
-    z_arrived(1)
-    project((1, 2), [z_recv[0], z_recv[1]], [pos_recv[0], pos_recv[1]])
+    near_arrived(1)
+    project_near(1)
 
     def frame_arrived(k, carry):
         j = lax.rem(tm + k, TM)
@@ -282,53 +302,102 @@
 
     lax.fori_loop(0, 64, widen, 0)
 
-    gather(1)
-    gather(2)
-    gather(3)
-
     def o_copy(j):
         return remote(o_send.at[j], o_recv.at[space], o_ssem.at[j], o_rsem.at[space], space=j)
 
     pair_row = lax.broadcasted_iota(jnp.int32, (PAIR, 2 * PATCHES), 0) < HD
-    chunks = [slice(n * CHUNK, (n + 1) * CHUNK) for n in range(KEYS // CHUNK)]
-
-    def attend(n, carry):
-        c = jnp.where(n < 4, 2 - n // 2, jnp.where(n < 6, 3, 0))
-        off = jnp.where(c == 3, 2, jnp.where(c == 2, 3, c))
-        first = lax.rem(n + x // 2 + 1, 2) * 2
-        queries = jnp.concatenate([x_recv[c, first, 0:PAIR], x_recv[c, first + 1, 0:PAIR]], axis=1)
+    heads = ((key_a, score_a), (key_b, score_b))
+
+    def queries_of(first, second):
+        return jnp.concatenate(
+            [x_recv[first[0], first[1], 0:PAIR], x_recv[second[0], second[1], 0:PAIR]], axis=1
+        )
+
+    def score(queries, blocks):
         tops = []
-        for keys, scores in ((key_a, score_a), (key_b, score_b)):
+        for keys, scores in heads:
             top = None
-            for rows in chunks:
+            for n in blocks:
+                rows = slice(n * CHUNK, (n + 1) * CHUNK)
                 product = matmul(keys[rows], queries)
                 scores[rows] = product
                 high = jnp.max(product.reshape(CHUNK // 8, 8, 2 * PATCHES), axis=0)
                 top = high if top is None else jnp.maximum(top, high)
             tops.append(jnp.max(top, axis=0, keepdims=True))
-        mixed = []
-        for scores, top in zip((score_a, score_b), tops):
+        return tops
+
+    def mix(tops, blocks):
+        sums = []
+        for (_, scores), top in zip(heads, tops):
             both = None
-            for rows in chunks:
+            for n in blocks:
+                rows = slice(n * CHUNK, (n + 1) * CHUNK)
                 weights = jnp.exp2((scores[rows] - top) * FACTOR).astype(BF16)
                 product = matmul(value_t[:, rows], weights)
                 both = product if both is None else both + product
-            mixed.append(both[0:PAIR] / both[PAIR : PAIR + 1])
-        result = jnp.where(pair_row, mixed[0], mixed[1]).astype(BF16)
+            sums.append(both)
+        return sums
+
+    def early(column, carry):
+        tops = score(queries_of((1, column), (2, column)), (0, 1, 2))
+        for h, (top, both) in enumerate(zip(tops, mix(tops, (0, 1, 2)))):
+            early_top[column, h] = jnp.broadcast_to(top, (8, 2 * PATCHES))
+            early_sum[column, h] = both
+        return carry
+
+    def divided(sums):
+        mixed = [both[0:PAIR] / both[PAIR : PAIR + 1] for both in sums]
+        return jnp.where(pair_row, mixed[0], mixed[1])
+
+    def finish_near(n, carry):
+        column = lax.rem(x + n, 4)
+        tops = []
+        scales = []
+        for h, top in enumerate(score(queries_of((1, column), (2, column)), (3,))):
+            old = early_top[column, h, 0:1]
+            tops.append(jnp.maximum(old, top))
+            scales.append(jnp.exp2((old - tops[h]) * FACTOR))
+        result = divided(
+            [both + early_sum[column, h] * scales[h] for h, both in enumerate(mix(tops, (3,)))]
+        )
+        for slot in range(2):
+            j = lax.rem(zh + (1, 3)[slot], 4) * 4 + column
+            low = slot * SIDE
+            o_send[j] = jnp.concatenate(
+                [result[:, low : low + SIDE], result[:, low + 2 * SIDE : low + 3 * SIDE]], axis=1
+            ).astype(BF16)
+            o_copy(j).start()
+        return carry
+
+    def finish_whole(c, n):
+        first = lax.rem(n + x // 2 + 1, 2) * 2
+        blocks = (0, 1, 2, 3)
+        result = divided(mix(score(queries_of((c, first), (c, first + 1)), blocks), blocks)).astype(BF16)
         for e in range(2):
-            j = lax.rem(zh + off, 4) * 4 + first + e
+            j = lax.rem(zh + 2, 4) * 4 + first + e if c else zh * 4 + first + e
             o_send[j] = result[:, e * PATCHES : (e + 1) * PATCHES]
-
-            @pl.when(j != space)
-            def _():
+            if c:
                 o_copy(j).start()
-
-        return carry
-
-    lax.fori_loop(0, 4, attend, 0)
+            else:
+
+                @pl.when(j != space)
+                def _():
+                    o_copy(j).start()
+
+    gather(1)
+    gather(2)
+    lax.fori_loop(0, 4, early, 0)
+    gather(3)
+    lax.fori_loop(0, 4, finish_near, 0)
     for k in range(4):
         x_arrived(3, lax.rem(x + k, 4), 1)
-    lax.fori_loop(4, 8, attend, 0)
+    for c in (3, 0):
+
+        def step(n, carry, c=c):
+            finish_whole(c, n)
+            return carry
+
+        lax.fori_loop(0, 2, step, 0)
     o_recv[space] = o_send[space]
 
     def t_copy(i, d):
@@ -445,7 +514,7 @@
     for store in stores:
         store.wait()
     for n in range(2):
-        z_copy(n)[1].wait_send()
+        pos_copy(n).wait_send()
     for c in range(4):
         for k in range(0 if c == 3 else 1, 4):
             for copy in x_copies(c, k):
@@ -489,6 +558,8 @@
         ((PAIR + 16, KEYS), BF16),
         ((KEYS, 2 * PATCHES), F32),
         ((KEYS, 2 * PATCHES), F32),
+        ((4, 2, 8, 2 * PATCHES), F32),
+        ((4, 2, PAIR + 16, 2 * PATCHES), F32),
         ((SPACE, PAIR, PATCHES), BF16),
         ((SPACE, PAIR, PATCHES), BF16),
         ((2, TM, 16, D), BF16),
@@ -499,7 +570,7 @@
         ((2, TM, 16, WIDE), BF16),
         ((FRAMES, PATCHES, D), BF16),
     ]
-    sems = [(20,), (2,), (2,), (2,), (2,), (TM,), (TM,), (5, 4), (5, 4)]
+    sems = [(20,), (2, 2), (2, 2), (2,), (2,), (TM,), (TM,), (5, 4), (5, 4)]
     sems += [(SPACE,), (SPACE,), (2, TM), (2, TM), (TM,), (TM,)]
     return pl.pallas_call(
         kernel,

time: 104 us -> 106 us (1.019)
  Pallas kernels: 101 us -> 104 us
    pallas_call x1, Pallas kernels: 101 us -> 104 us  [block(): pl.pallas_call(kernel, out_shape=jax.ShapeDtypeStruct((FRAMES, PATCHES, D...]
where the time goes in v8:
time: 106 us
  Pallas kernels  104 us (98%)
  local copies, waits for them, and re-layouts  2.37 us (2%)
    pallas_call x1, Pallas kernels, block(): pl.pallas_call(kernel, out_shape=jax.ShapeDtypeStruct((FRAMES, PATCHES, D...  104 us
    unnamed x1, local copies, waits for them, and re-layouts  2.37 us

profile of v8, /device:TPU:1, one launch (start us, length us, event | category | flops | bytes accessed | tf_op | source)
XLA Modules:
  0.0 106.2 jit_solution(981052537741458437)
XLA Ops:
  0.0 103.8 %space_time_block.1 = bf16[4,128,1152]{2,1,0:T(8,128)(2,1)} custom-call(bf16[4,128,1152]{2,1,0:T(8,128)(2,1)} %video.1, s32[128]{0:T(128)} %row_index_in.1, s32[128]{0:T(128)} %col_index_in.1, s32[4]{0:T(128)} %frame_index.1, f32[1152]{0:T(1024)} %shift_s_in.1, f32[1152]{0:T(1024)} %scale_s_in.1, f32[1152]{0:T(1024)} %gate_s_in.1, ...), custom_call_target="tpu_custom_call" | custom-call | tf_op jit(solution)/shard_map/space_time_block/pallas_call | solution.py:575
  103.8 2.4 %copy.18 = bf16[4,128,1152]{2,1,0:T(8,128)(2,1)} copy(bf16[4,128,1152]{2,1,0:T(8,128)(2,1)} %space_time_block.1) | data formatting | bytes 2359296

commit v9 on v8

--- a/solution.py
+++ b/solution.py
@@ -268,39 +268,11 @@
     for part in range(2):
         for k in range(4):
             x_copies(3, k)[part].start()
-    for k in range(1, TM):
-        frame_copy(k).start()
     near_arrived(1)
     project_near(1)
 
-    def frame_arrived(k, carry):
-        j = lax.rem(tm + k, TM)
-        remote(frame_recv.at[tm], frame_recv.at[j], f_ssem.at[j], f_rsem.at[j], tm=j).wait_recv()
-        return carry
-
-    lax.fori_loop(1, TM, frame_arrived, 0)
-
     def side(s):
         return lax.rem(zl + s, 2) * NEAR
-
-    for s in range(2):
-        for n in range(NEAR):
-            for i in range(2):
-                at = s * 32 + i * 16 + n * 2
-                frame_rows[at : at + 2] = frame_recv[side(s) + n, 2 * i : 2 * i + 2]
-    angles = frame_rows[:, 0:1] * table_t[0:1, :]
-    sine = jnp.sin(angles)
-    time_rows[0] = jnp.cos(angles)
-    time_rows[1] = sine * table_t[1:2, :]
-    time_rows[2] = sine * table_t[2:3, :]
-
-    def widen(g, carry):
-        rows = pl.ds(pl.multiple_of(g * 8, 8), 8)
-        for n in range(3):
-            time_tables[n, rows] = jnp.broadcast_to(time_rows[n, pl.ds(g, 1)], (8, WIDE))
-        return carry
-
-    lax.fori_loop(0, 64, widen, 0)
 
     def o_copy(j):
         return remote(o_send.at[j], o_recv.at[space], o_ssem.at[j], o_rsem.at[space], space=j)
@@ -399,6 +371,8 @@
 
         lax.fori_loop(0, 2, step, 0)
     o_recv[space] = o_send[space]
+    for k in range(1, TM):
+        frame_copy(k).start()
 
     def t_copy(i, d):
         return remote(t_send.at[i, d], t_recv.at[i, tm], t_ssem.at[i, d], t_rsem.at[i, tm], tm=d)
@@ -435,6 +409,32 @@
         for s, r in peers:
             t_copy(i, peer(s, r)).start()
         t_recv[i, tm] = t_send[i, tm]
+
+    def frame_arrived(k, carry):
+        j = lax.rem(tm + k, TM)
+        remote(frame_recv.at[tm], frame_recv.at[j], f_ssem.at[j], f_rsem.at[j], tm=j).wait_recv()
+        return carry
+
+    lax.fori_loop(1, TM, frame_arrived, 0)
+
+    for s in range(2):
+        for n in range(NEAR):
+            for i in range(2):
+                at = s * 32 + i * 16 + n * 2
+                frame_rows[at : at + 2] = frame_recv[side(s) + n, 2 * i : 2 * i + 2]
+    angles = frame_rows[:, 0:1] * table_t[0:1, :]
+    sine = jnp.sin(angles)
+    time_rows[0] = jnp.cos(angles)
+    time_rows[1] = sine * table_t[1:2, :]
+    time_rows[2] = sine * table_t[2:3, :]
+
+    def widen(g, carry):
+        rows = pl.ds(pl.multiple_of(g * 8, 8), 8)
+        for n in range(3):
+            time_tables[n, rows] = jnp.broadcast_to(time_rows[n, pl.ds(g, 1)], (8, WIDE))
+        return carry
+
+    lax.fori_loop(0, 64, widen, 0)
 
     for copy in load_w_t:
         copy.wait()

time: 106 us -> 96.2 us (0.908)
  Pallas kernels: 104 us -> 93.7 us
    pallas_call x1, Pallas kernels: 104 us -> 93.7 us  [block(): pl.pallas_call(kernel, out_shape=jax.ShapeDtypeStruct((FRAMES, PATCHES, D...]
where the time goes in v9:
time: 96.2 us; the launch traced here: 96.1 us
  Pallas kernels  93.7 us (97%)
  local copies, waits for them, and re-layouts  2.37 us (2%)
    pallas_call x1, Pallas kernels, block(): pl.pallas_call(kernel, out_shape=jax.ShapeDtypeStruct((FRAMES, PATCHES, D...  93.7 us
    unnamed x1, local copies, waits for them, and re-layouts  2.37 us

profile of v9, /device:TPU:1, one launch (start us, length us, event | category | flops | bytes accessed | tf_op | source)
XLA Modules:
  0.0 96.1 jit_solution(14471123933385355374)
XLA Ops:
  0.0 93.7 %space_time_block.1 = bf16[4,128,1152]{2,1,0:T(8,128)(2,1)} custom-call(bf16[4,128,1152]{2,1,0:T(8,128)(2,1)} %video.1, s32[128]{0:T(128)} %row_index_in.1, s32[128]{0:T(128)} %col_index_in.1, s32[4]{0:T(128)} %frame_index.1, f32[1152]{0:T(1024)} %shift_s_in.1, f32[1152]{0:T(1024)} %scale_s_in.1, f32[1152]{0:T(1024)} %gate_s_in.1, ...), custom_call_target="tpu_custom_call" | custom-call | tf_op jit(solution)/shard_map/space_time_block/pallas_call | solution.py:575
  93.7 2.4 %copy.18 = bf16[4,128,1152]{2,1,0:T(8,128)(2,1)} copy(bf16[4,128,1152]{2,1,0:T(8,128)(2,1)} %space_time_block.1) | data formatting | bytes 2359296

commit v10 on v9

--- a/solution.py
+++ b/solution.py
@@ -385,9 +385,10 @@
     for copy in load_rest:
         copy.wait()
     load_out_s.wait()
-    for i in range(2):
-
-        def o_arrived(n, carry):
+    for late in range(2):
+        i = lax.rem(zh // 2 + late, 2)
+
+        def o_arrived(n, carry, i=i):
             j = i * 8 + n
 
             @pl.when(j != space)
@@ -400,10 +401,10 @@
         mixed = []
         for e in range(2):
             f = 2 * i + e
-            attended = o_recv[4 * f : 4 * f + 4].reshape(INNER, PATCHES)
+            attended = o_recv[pl.ds(4 * f, 4)].reshape(INNER, PATCHES)
             mixed.append(jnp.transpose(attended.astype(F32)).astype(BF16))
         branch = matmul(jnp.concatenate(mixed, axis=0), out_s_held[...])
-        stream = video_held[2 * i : 2 * i + 2].reshape(2 * PATCHES, D).astype(F32)
+        stream = video_held[pl.ds(2 * i, 2)].reshape(2 * PATCHES, D).astype(F32)
         stream = (stream + gate_s[...].reshape(1, D) * branch).reshape(2, TM, 8, D)
         t_send[i] = jnp.stack([stream[0], stream[1]], axis=1).reshape(TM, 16, D).astype(BF16)
         for s, r in peers:

time: 96.2 us -> 96.3 us (level)
  no operation moved by 1% of the time
where the time goes in v10:
time: 96.3 us; the launch traced here: 96.1 us
  Pallas kernels  93.8 us (97%)
  local copies, waits for them, and re-layouts  2.37 us (2%)
    pallas_call x1, Pallas kernels, block(): pl.pallas_call(kernel, out_shape=jax.ShapeDtypeStruct((FRAMES, PATCHES, D...  93.8 us
    unnamed x1, local copies, waits for them, and re-layouts  2.37 us

profile of v10, /device:TPU:1, one launch (start us, length us, event | category | flops | bytes accessed | tf_op | source)
XLA Modules:
  0.0 96.1 jit_solution(16145679813215046126)
XLA Ops:
  0.0 93.8 %space_time_block.1 = bf16[4,128,1152]{2,1,0:T(8,128)(2,1)} custom-call(bf16[4,128,1152]{2,1,0:T(8,128)(2,1)} %video.1, s32[128]{0:T(128)} %row_index_in.1, s32[128]{0:T(128)} %col_index_in.1, s32[4]{0:T(128)} %frame_index.1, f32[1152]{0:T(1024)} %shift_s_in.1, f32[1152]{0:T(1024)} %scale_s_in.1, f32[1152]{0:T(1024)} %gate_s_in.1, ...), custom_call_target="tpu_custom_call" | custom-call | tf_op jit(solution)/shard_map/space_time_block/pallas_call | solution.py:576
  93.8 2.4 %copy.18 = bf16[4,128,1152]{2,1,0:T(8,128)(2,1)} copy(bf16[4,128,1152]{2,1,0:T(8,128)(2,1)} %space_time_block.1) | data formatting | bytes 2359296
